TPU v7x, 256 devices: a whole 4x4x8 slice. The times are simulated.
256 devices in a mesh: mem: 16 (over x_lo, y, core), lon: 16 (over z, x_hi).
Axes of the slice: x: 4 (x_hi: 2, x_lo: 2; x = x_hi * 2 + x_lo), y: 4, z: 8, core: 2. Of those that a mesh axis runs over, the one named last changes fastest.
Arguments:
- members: bfloat16 [32, 32, 32, 2048], P('mem', None, None, 'lon'), may hold values from -6 to 6
- conv_one: bfloat16 [32, 32, 5, 5], replicated, may hold values from -0.21875 to 0.21875
- conv_two: bfloat16 [32, 32, 5, 5], replicated, may hold values from -0.21875 to 0.21875
- conv_three: bfloat16 [32, 32, 5, 5], replicated, may hold values from -0.21875 to 0.21875
- norm_gain: float32 [32], replicated, may hold values from 0.1 to 1.9
- w_query: bfloat16 [32, 32], replicated, may hold values from -9 to 9
- w_key: bfloat16 [32, 32], replicated, may hold values from -1 to 1
- w_value: bfloat16 [32, 32], replicated, may hold values from -1 to 1
- w_out: bfloat16 [32, 32], replicated, may hold values from -1 to 1
Outputs:
- ensemble_out: bfloat16 [32, 32, 32, 2048], P('mem', None, None, 'lon')
All inputs are finite; a program needn't handle non-finite values.
Results may differ from a plain program's by a relative error of at most 0.03.
Values may be sent and summed in bfloat16 or wider, within the bound.
A program may use at most 64 MiB of HBM per device.

v0:
```python
import math

import jax
import jax.numpy as jnp
from jax import lax
from jax.experimental import pallas as pl
from jax.experimental.pallas import tpu as pltpu
from jax.sharding import PartitionSpec as P

MESH = pl.DeviceIdType.MESH
HEADS = 4
BF = jnp.bfloat16
F32 = jnp.float32
PEERS = 16


def iota(shape, dim):
    return lax.broadcasted_iota(jnp.int32, shape, dim)


def ones_where(mask):
    return jnp.where(mask, 1.0, 0.0).astype(BF)


def dot(a, b, contract=((1,), (0,))):
    return lax.dot_general(a, b, (contract, ((), ())), preferred_element_type=F32)


def device(**where):
    return {name: index for name, index in where.items()}


def kernel(
    x_ref,
    w1_ref,
    w2_ref,
    w3_ref,
    gain_ref,
    wq_ref,
    wk_ref,
    wv_ref,
    wo_ref,
    out_ref,
    z_ref,
    xa_ref,
    xb_ref,
    xc_ref,
    band_ref,
    proj_ref,
    back_ref,
    gcol_ref,
    hs_ref,
    hr_ref,
    send_ref,
    recv_ref,
    q_ref,
    k_ref,
    v_ref,
    s_ref,
    mix_ref,
    ret_ref,
    got_ref,
    halo_send,
    halo_recv,
    go_send,
    go_recv,
    back_send,
    back_recv,
):
    me = lax.axis_index("mem")
    col = lax.axis_index("lon")
    right, left = lax.rem(col + 1, PEERS), lax.rem(col + PEERS - 1, PEERS)

    barrier = pltpu.get_barrier_semaphore()

    def greet(step, carry):
        pl.semaphore_signal(
            barrier, inc=1, device_id={"mem": lax.rem(me + step, PEERS)}, device_id_type=MESH
        )
        return carry

    for side in (left, right):
        pl.semaphore_signal(barrier, inc=1, device_id={"lon": side}, device_id_type=MESH)
    lax.fori_loop(1, PEERS, greet, 0)

    for m in range(2):
        z_ref[m] = x_ref[m].astype(F32).reshape(1024, 128)
    for buf in (xa_ref, xb_ref, xc_ref):
        buf[0:64, :] = jnp.zeros((64, 384), BF)
        buf[1088:1152, :] = jnp.zeros((64, 384), BF)
    for m in range(2):
        for lat in range(32):
            rows = z_ref[m, pl.ds(lat, 32, stride=32), :]
            xa_ref[64 + 32 * lat : 96 + 32 * lat, 128 * m : 128 * m + 128] = rows.astype(BF)

    r, lane = iota((32, 256), 0), iota((32, 256), 1)
    want = jnp.where(r < 16, 0, 120) + (r & 7) + jnp.where((r & 8) != 0, 128, 0)
    edges = dot(ones_where(lane == want), xa_ref[64:1088, 0:256], ((1,), (1,)))
    edges = edges.astype(BF)
    hs_ref[0] = edges[0:16]
    hs_ref[1] = edges[16:32]

    pl.semaphore_wait(barrier, PEERS + 1)

    def halo(side, target):
        return pltpu.make_async_remote_copy(
            src_ref=hs_ref.at[side],
            dst_ref=hr_ref.at[side],
            send_sem=halo_send.at[side],
            recv_sem=halo_recv.at[side],
            device_id={"lon": target},
            device_id_type=MESH,
        )

    to_left, to_right = halo(0, left), halo(1, right)
    to_left.start()
    to_right.start()

    for layer, w_ref in enumerate((w1_ref, w2_ref, w3_ref)):
        for dx in range(5):
            pieces = [w_ref[dy, dx].astype(F32) for dy in range(5)]
            base = jnp.concatenate(pieces + [jnp.zeros((32, 96), F32)], axis=1)
            for up in range(4):
                rolled = base if up == 0 else pltpu.roll(base, 32 * up, 1)
                at = dx * 128 + up * 32
                band_ref[layer, at : at + 32, :] = rolled.astype(BF)

    r, c = iota((256, 32), 0), iota((256, 32), 1)
    spread = ones_where((r >> 3) == c)
    spread_out = ones_where((r & 31) == c)
    c, lane = iota((32, 256), 0), iota((32, 256), 1)
    tile = ones_where((lane & 31) == c)
    tile_out = ones_where((lane >> 3) == c)
    r, lane = iota((256, 256), 0), iota((256, 256), 1)
    own = (r & 7) == (lane >> 5)
    own_out = (r >> 5) == (lane & 7)
    for index, w_ref in enumerate((wq_ref, wk_ref, wv_ref)):
        tall = dot(spread, w_ref[...], ((1,), (1,))).astype(BF)
        full = jnp.where(own, dot(tall, tile), 0.0)
        proj_ref[256 * index : 256 * index + 256, :] = full.astype(BF)
    tall = dot(spread_out, wo_ref[...], ((1,), (1,))).astype(BF)
    back_ref[...] = jnp.where(own_out, dot(tall, tile_out), 0.0).astype(BF)
    eye = iota((32, 32), 0) == iota((32, 32), 1)
    gains = jnp.broadcast_to(gain_ref[...], (32, 32))
    gcol = jnp.sum(jnp.where(eye, gains, 0.0), axis=1, keepdims=True)
    gcol_ref[...] = jnp.broadcast_to(gcol, (32, 128))

    to_left.wait()
    to_right.wait()

    r, lane = iota((256, 128), 0), iota((256, 128), 1)
    lon, base = r & 127, (r >> 7) * 64
    inner = jnp.where(lon < 16, base + 16 + lon, jnp.where(lon >= 112, base + lon - 80, -1))
    r2, lane2 = iota((32, 128), 0), iota((32, 128), 1)
    outer = jnp.where(r2 < 16, 48, 8) + (r2 & 7) + jnp.where((r2 & 8) != 0, 64, 0)
    strip = dot(xa_ref[64:1088, 0:256], ones_where(lane == inner))
    ring = hr_ref[...].reshape(32, 1024)
    strip = strip + dot(ring, ones_where(lane2 == outer), ((0,), (0,)))
    xa_ref[64:1088, 256:384] = strip.astype(BF)

    def convolve(source, layer, block):
        window = source[pl.ds(pl.multiple_of(block * 128, 128), 256), :]
        total = [None, None, None]
        for dx in range(5):
            y = dot(band_ref[layer, dx * 128 : dx * 128 + 128, :], window)
            for t in range(3):
                part = y[:, 128 * t : 128 * t + 128]
                if dx != 2:
                    part = pltpu.roll(part, (2 - dx) % 128, 1)
                total[t] = part if total[t] is None else total[t] + part
        return total

    def silu_layer(source, target, layer):
        def body(block, carry):
            total = convolve(source, layer, block)
            at = pl.ds(pl.multiple_of(64 + block * 128, 64), 128)
            for t in range(3):
                value = 0.5 * total[t]
                value = value * jnp.tanh(value) + value
                target[at, 128 * t : 128 * t + 128] = value.astype(BF)
            return carry

        lax.fori_loop(0, 8, body, 0)

    silu_layer(xa_ref, xb_ref, 0)
    silu_layer(xb_ref, xc_ref, 1)

    def go(slot, peer):
        return pltpu.make_async_remote_copy(
            src_ref=send_ref.at[16 * slot + peer],
            dst_ref=recv_ref.at[slot, me],
            send_sem=go_send.at[slot, peer],
            recv_sem=go_recv.at[slot, me],
            device_id={"mem": peer},
            device_id_type=MESH,
        )

    def last_layer(step, carry):
        slot = step // 4
        quarter = lax.rem(step + me // 4, 4)
        block = slot * 4 + quarter
        total = convolve(xc_ref, 2, block)
        at = pl.ds(pl.multiple_of(64 + block * 128, 64), 128)
        state = []
        for t in range(3):
            value = total[t] + xa_ref[at, 128 * t : 128 * t + 128].astype(F32)
            state.append(value.astype(BF).astype(F32))
        lane = iota((128, 128), 1)
        for m in range(2):
            low = pltpu.roll(state[2], 112 - 64 * m, 1)
            high = pltpu.roll(state[2], (80 - 64 * m) % 128, 1)
            whole = jnp.where(lane < 8, low, jnp.where(lane >= 120, high, state[m]))
            whole = whole.astype(BF)
            for row in range(4):
                send_ref[4 * block + row, m] = whole[32 * row : 32 * row + 32]
        for row in range(4):
            peer = quarter * 4 + row

            @pl.when(peer != me)
            def _():
                go(slot, peer).start()

            @pl.when(peer == me)
            def _():
                recv_ref[slot, me] = send_ref[16 * slot + me]

        return carry

    lax.fori_loop(0, 8, last_layer, 0)

    scale = math.log2(math.e) / math.sqrt(32 // HEADS)

    def back(slot, peer):
        return pltpu.make_async_remote_copy(
            src_ref=ret_ref.at[slot, peer],
            dst_ref=got_ref.at[16 * slot + me],
            send_sem=back_send.at[slot, peer],
            recv_sem=back_recv.at[slot, me],
            device_id={"mem": peer},
            device_id_type=MESH,
        )

    def attend(slot, carry):
        def arrived(step, carry):
            peer = lax.rem(me + step, PEERS)
            pltpu.make_async_remote_copy(
                src_ref=send_ref.at[16 * slot + peer],
                dst_ref=recv_ref.at[slot, peer],
                send_sem=go_send.at[slot, peer],
                recv_sem=go_recv.at[slot, peer],
                device_id={"mem": peer},
                device_id_type=MESH,
            ).wait_recv()
            return carry

        lax.fori_loop(1, PEERS, arrived, 0)

        def prepare(group, carry):
            values = recv_ref[slot, pl.ds(4 * group, 4)].astype(F32).reshape(8, 32, 128)
            centred = values - jnp.mean(values, axis=1, keepdims=True)
            spread = jnp.mean(centred * centred, axis=1, keepdims=True)
            normed = centred * lax.rsqrt(spread + 1e-05) * gcol_ref[...][None]
            out = dot(proj_ref[...], normed.astype(BF).reshape(256, 128))
            out = out.astype(BF).astype(F32)
            q_ref[group] = (out[0:256] * scale).reshape(32, 8, 128)
            k_ref[group] = out[256:512].reshape(32, 8, 128)
            v_ref[group] = out[512:768].reshape(32, 8, 128)
            return carry

        lax.fori_loop(0, 4, prepare, 0)

        def head(h, carry):
            queries = [[q_ref[mb, 8 * h + d] for mb in range(4)] for d in range(8)]

            def score(group, peak):
                peak = list(peak)
                for n in range(8):
                    total = [None] * 4
                    for d in range(8):
                        key = jnp.broadcast_to(k_ref[group, 8 * h + d, n : n + 1, :], (8, 128))
                        for mb in range(4):
                            term = queries[d][mb] * key
                            total[mb] = term if d == 0 else total[mb] + term
                    for mb in range(4):
                        s_ref[8 * group + n, mb] = total[mb]
                        peak[mb] = jnp.maximum(peak[mb], total[mb])
                return tuple(peak)

            low = jnp.full((8, 128), -jnp.inf, F32)
            peak = lax.fori_loop(0, 4, score, (low,) * 4)

            def mix(group, state):
                weight, mixed = list(state[0]), [list(m) for m in state[1]]
                for n in range(8):
                    probs = [jnp.exp2(s_ref[8 * group + n, mb] - peak[mb]) for mb in range(4)]
                    for mb in range(4):
                        weight[mb] = weight[mb] + probs[mb]
                    for d in range(8):
                        value = jnp.broadcast_to(v_ref[group, 8 * h + d, n : n + 1, :], (8, 128))
                        for mb in range(4):
                            mixed[d][mb] = mixed[d][mb] + probs[mb] * value
                return tuple(weight), tuple(tuple(m) for m in mixed)

            zero = jnp.zeros((8, 128), F32)
            weight, mixed = lax.fori_loop(0, 4, mix, ((zero,) * 4, ((zero,) * 4,) * 8))
            for mb in range(4):
                inverse = 1.0 / weight[mb]
                for d in range(8):
                    mix_ref[mb, 8 * h + d] = mixed[d][mb] * inverse
            return carry

        lax.fori_loop(0, HEADS, head, 0)

        def finish(group, carry):
            mixed = mix_ref[group].reshape(256, 128).astype(BF)
            state = recv_ref[slot, pl.ds(4 * group, 4)].astype(F32).reshape(256, 128)
            final = dot(back_ref[...], mixed) + state
            ret_ref[slot, pl.ds(4 * group, 4)] = final.astype(BF).reshape(4, 2, 32, 128)
            for row in range(4):
                peer = 4 * group + row

                @pl.when(peer != me)
                def _():
                    back(slot, peer).start()

                @pl.when(peer == me)
                def _():
                    got_ref[16 * slot + me] = ret_ref[slot, me]

            return carry

        lax.fori_loop(0, 4, finish, 0)
        return carry

    lax.fori_loop(0, 2, attend, 0)

    def returned(slot, carry):
        def one(step, carry):
            peer = lax.rem(me + step, PEERS)
            pltpu.make_async_remote_copy(
                src_ref=ret_ref.at[slot, peer],
                dst_ref=got_ref.at[16 * slot + peer],
                send_sem=back_send.at[slot, peer],
                recv_sem=back_recv.at[slot, peer],
                device_id={"mem": peer},
                device_id_type=MESH,
            ).wait_recv()
            return carry

        lax.fori_loop(1, PEERS, one, 0)

        def place(lat, carry):
            for m in range(2):
                z_ref[m, pl.ds(16 * slot + lat, 32, stride=32), :] = got_ref[
                    16 * slot + lat, m
                ].astype(F32)
            return carry

        lax.fori_loop(0, 16, place, 0)
        return carry

    lax.fori_loop(0, 2, returned, 0)
    for m in range(2):
        out_ref[m] = z_ref[m].astype(BF).reshape(32, 32, 128)

    def sent(step, carry):
        peer = lax.rem(me + step, PEERS)
        for slot in range(2):
            go(slot, peer).wait_send()
            back(slot, peer).wait_send()
        return carry

    lax.fori_loop(1, PEERS, sent, 0)


def on_device(members, conv_one, conv_two, conv_three, norm_gain, w_query, w_key, w_value, w_out):
    taps = [jnp.transpose(w, (2, 3, 0, 1)) for w in (conv_one, conv_two, conv_three)]
    vmem = pl.BlockSpec(memory_space=pltpu.VMEM)
    return pl.pallas_call(
        kernel,
        out_shape=jax.ShapeDtypeStruct(members.shape, BF),
        in_specs=[vmem] * 9,
        out_specs=vmem,
        scratch_shapes=[
            pltpu.VMEM((2, 1024, 128), F32),
            pltpu.VMEM((1152, 384), BF),
            pltpu.VMEM((1152, 384), BF),
            pltpu.VMEM((1152, 384), BF),
            pltpu.VMEM((3, 640, 256), BF),
            pltpu.VMEM((768, 256), BF),
            pltpu.VMEM((256, 256), BF),
            pltpu.VMEM((32, 128), F32),
            pltpu.VMEM((2, 16, 1024), BF),
            pltpu.VMEM((2, 16, 1024), BF),
            pltpu.VMEM((32, 2, 32, 128), BF),
            pltpu.VMEM((2, 16, 2, 32, 128), BF),
            pltpu.VMEM((4, 32, 8, 128), F32),
            pltpu.VMEM((4, 32, 8, 128), F32),
            pltpu.VMEM((4, 32, 8, 128), F32),
            pltpu.VMEM((32, 4, 8, 128), F32),
            pltpu.VMEM((4, 32, 8, 128), F32),
            pltpu.VMEM((2, 16, 2, 32, 128), BF),
            pltpu.VMEM((32, 2, 32, 128), BF),
            pltpu.SemaphoreType.DMA((2,)),
            pltpu.SemaphoreType.DMA((2,)),
            pltpu.SemaphoreType.DMA((2, 16)),
            pltpu.SemaphoreType.DMA((2, 16)),
            pltpu.SemaphoreType.DMA((2, 16)),
            pltpu.SemaphoreType.DMA((2, 16)),
        ],
        compiler_params=pltpu.CompilerParams(
            collective_id=0, has_side_effects=True, vmem_limit_bytes=40 * 1024 * 1024
        ),
    )(members, *taps, norm_gain.reshape(1, 32), w_query, w_key, w_value, w_out)


def solution(mesh):
    in_specs = (P("mem", None, None, "lon"), P(), P(), P(), P(), P(), P(), P(), P())
    out_specs = P("mem", None, None, "lon")
    return jax.shard_map(
        on_device, mesh=mesh, in_specs=in_specs, out_specs=out_specs, check_vma=False
    )
```

profile of v0, /device:TPU:1, one launch (start us, length us, event | category | flops | bytes accessed | tf_op | source)
XLA Modules:
  0.0 53.4 jit_solution(11172565875265470237)
XLA Ops:
  0.0 0.0 copy-start.8
  0.0 0.7 %copy-done.8 = f32[32]{0:T(128)S(1)} copy-done((f32[32]{0:T(128)S(1)}, f32[32]{0:T(128)}, u32[]{:S(2)}) %copy-start.8) | copy-done | bytes 152
  0.7 0.0 copy-start
  0.7 1.0 %copy-done = bf16[2,32,32,128]{3,2,1,0:T(8,128)(2,1)S(1)} copy-done((bf16[2,32,32,128]{3,2,1,0:T(8,128)(2,1)S(1)}, bf16[2,32,32,128]{3,2,1,0:T(8,128)(2,1)}, u32[]{:S(2)}) %copy-start) | copy-done | bytes 524312
  1.7 0.0 copy-start.1
  1.7 0.9 %copy-done.1 = bf16[32,32,5,5]{1,0,3,2:T(8,128)(2,1)S(1)} copy-done((bf16[32,32,5,5]{1,0,3,2:T(8,128)(2,1)S(1)}, bf16[32,32,5,5]{1,0,3,2:T(8,128)(2,1)}, u32[]{:S(2)}) %copy-start.1) | copy-done | bytes 51224
  2.6 0.0 copy-start.2
  2.6 0.9 %copy-done.2 = bf16[32,32,5,5]{1,0,3,2:T(8,128)(2,1)S(1)} copy-done((bf16[32,32,5,5]{1,0,3,2:T(8,128)(2,1)S(1)}, bf16[32,32,5,5]{1,0,3,2:T(8,128)(2,1)}, u32[]{:S(2)}) %copy-start.2) | copy-done | bytes 51224
  3.6 0.0 copy-start.3
  3.6 0.9 %copy-done.3 = bf16[32,32,5,5]{1,0,3,2:T(8,128)(2,1)S(1)} copy-done((bf16[32,32,5,5]{1,0,3,2:T(8,128)(2,1)S(1)}, bf16[32,32,5,5]{1,0,3,2:T(8,128)(2,1)}, u32[]{:S(2)}) %copy-start.3) | copy-done | bytes 51224
  4.5 0.0 copy-start.4
  4.5 0.7 %copy-done.4 = bf16[32,32]{1,0:T(8,128)(2,1)S(1)} copy-done((bf16[32,32]{1,0:T(8,128)(2,1)S(1)}, bf16[32,32]{1,0:T(8,128)(2,1)}, u32[]{:S(2)}) %copy-start.4) | copy-done | bytes 2072
  5.2 0.0 copy-start.5
  5.2 0.7 %copy-done.5 = bf16[32,32]{1,0:T(8,128)(2,1)S(1)} copy-done((bf16[32,32]{1,0:T(8,128)(2,1)S(1)}, bf16[32,32]{1,0:T(8,128)(2,1)}, u32[]{:S(2)}) %copy-start.5) | copy-done | bytes 2072
  5.9 0.0 copy-start.6
  5.9 0.7 %copy-done.6 = bf16[32,32]{1,0:T(8,128)(2,1)S(1)} copy-done((bf16[32,32]{1,0:T(8,128)(2,1)S(1)}, bf16[32,32]{1,0:T(8,128)(2,1)}, u32[]{:S(2)}) %copy-start.6) | copy-done | bytes 2072
  6.6 0.0 copy-start.7
  6.6 0.7 %copy-done.7 = bf16[32,32]{1,0:T(8,128)(2,1)S(1)} copy-done((bf16[32,32]{1,0:T(8,128)(2,1)S(1)}, bf16[32,32]{1,0:T(8,128)(2,1)}, u32[]{:S(2)}) %copy-start.7) | copy-done | bytes 2072
  7.3 45.3 %shard_map.91 = bf16[2,32,32,128]{3,2,1,0:T(8,128)(2,1)S(1)} custom-call(bf16[2,32,32,128]{3,2,1,0:T(8,128)(2,1)S(1)} %copy-done, bf16[5,5,32,32]{3,2,1,0:T(8,128)(2,1)S(1)} %bitcast.4, bf16[5,5,32,32]{3,2,1,0:T(8,128)(2,1)S(1)} %bitcast.5, bf16[5,5,32,32]{3,2,1,0:T(8,128)(2,1)S(1)} %bitcast.6, f32[1,32]{1,0:T(1,128)S(1)} %bitcast.7, ...), custom_call_target="tpu_custom_call" | custom-call | tf_op jit(solution)/shard_map/pallas_call | solution.py:379
  52.6 0.8 %copy.11 = bf16[2,32,32,128]{3,2,1,0:T(8,128)(2,1)} copy(bf16[2,32,32,128]{3,2,1,0:T(8,128)(2,1)S(1)} %shard_map.91) | data formatting | bytes 1048576
Async XLA Ops:
  0.0 0.7 %copy-start.8 = (f32[32]{0:T(128)S(1)}, f32[32]{0:T(128)}, u32[]{:S(2)}) copy-start(f32[32]{0:T(128)} %param.13) | copy-start | bytes 388
  0.7 1.0 %copy-start = (bf16[2,32,32,128]{3,2,1,0:T(8,128)(2,1)S(1)}, bf16[2,32,32,128]{3,2,1,0:T(8,128)(2,1)}, u32[]{:S(2)}) copy-start(bf16[2,32,32,128]{3,2,1,0:T(8,128)(2,1)} %x_ref.1) | copy-start | bytes 1572868
  1.7 0.9 %copy-start.1 = (bf16[32,32,5,5]{1,0,3,2:T(8,128)(2,1)S(1)}, bf16[32,32,5,5]{1,0,3,2:T(8,128)(2,1)}, u32[]{:S(2)}) copy-start(bf16[32,32,5,5]{1,0,3,2:T(8,128)(2,1)} %param.10) | copy-start | bytes 153604
  2.6 0.9 %copy-start.2 = (bf16[32,32,5,5]{1,0,3,2:T(8,128)(2,1)S(1)}, bf16[32,32,5,5]{1,0,3,2:T(8,128)(2,1)}, u32[]{:S(2)}) copy-start(bf16[32,32,5,5]{1,0,3,2:T(8,128)(2,1)} %param.11) | copy-start | bytes 153604
  3.6 0.9 %copy-start.3 = (bf16[32,32,5,5]{1,0,3,2:T(8,128)(2,1)S(1)}, bf16[32,32,5,5]{1,0,3,2:T(8,128)(2,1)}, u32[]{:S(2)}) copy-start(bf16[32,32,5,5]{1,0,3,2:T(8,128)(2,1)} %param.12) | copy-start | bytes 153604
  4.5 0.7 %copy-start.4 = (bf16[32,32]{1,0:T(8,128)(2,1)S(1)}, bf16[32,32]{1,0:T(8,128)(2,1)}, u32[]{:S(2)}) copy-start(bf16[32,32]{1,0:T(8,128)(2,1)} %wq_ref.1) | copy-start | bytes 6148
  5.2 0.7 %copy-start.5 = (bf16[32,32]{1,0:T(8,128)(2,1)S(1)}, bf16[32,32]{1,0:T(8,128)(2,1)}, u32[]{:S(2)}) copy-start(bf16[32,32]{1,0:T(8,128)(2,1)} %wk_ref.1) | copy-start | bytes 6148
  5.9 0.7 %copy-start.6 = (bf16[32,32]{1,0:T(8,128)(2,1)S(1)}, bf16[32,32]{1,0:T(8,128)(2,1)}, u32[]{:S(2)}) copy-start(bf16[32,32]{1,0:T(8,128)(2,1)} %wv_ref.1) | copy-start | bytes 6148
  6.6 0.7 %copy-start.7 = (bf16[32,32]{1,0:T(8,128)(2,1)S(1)}, bf16[32,32]{1,0:T(8,128)(2,1)}, u32[]{:S(2)}) copy-start(bf16[32,32]{1,0:T(8,128)(2,1)} %wo_ref.1) | copy-start | bytes 6148
where the time goes:
time: 53.7 us; the launch traced here: 53.4 us
  Pallas kernels  45.3 us (84%)
  local copies, waits for them, and re-layouts  8.07 us (15%)
    pallas_call x1, Pallas kernels, on_device(): pl.pallas_call(kernel, out_shape=jax.ShapeDtypeStruct(members.shape, BF),...  45.3 us
    unnamed x19, local copies, waits for them, and re-layouts  8.07 us

commit v1 on v0

--- a/solution.py
+++ b/solution.py
@@ -31,6 +31,16 @@
 
 
 def kernel(
+    x_hbm,
+    w1_hbm,
+    w2_hbm,
+    w3_hbm,
+    gain_hbm,
+    wq_hbm,
+    wk_hbm,
+    wv_hbm,
+    wo_hbm,
+    out_ref,
     x_ref,
     w1_ref,
     w2_ref,
@@ -40,7 +50,6 @@
     wk_ref,
     wv_ref,
     wo_ref,
-    out_ref,
     z_ref,
     xa_ref,
     xb_ref,
@@ -66,7 +75,26 @@
     go_recv,
     back_send,
     back_recv,
+    load_sem,
 ):
+    loads = [
+        pltpu.make_async_copy(source, target, load_sem.at[index])
+        for index, (source, target) in enumerate(
+            (
+                (x_hbm, x_ref),
+                (w1_hbm, w1_ref),
+                (w2_hbm, w2_ref),
+                (w3_hbm, w3_ref),
+                (gain_hbm, gain_ref),
+                (wq_hbm, wq_ref),
+                (wk_hbm, wk_ref),
+                (wv_hbm, wv_ref),
+                (wo_hbm, wo_ref),
+            )
+        )
+    ]
+    for load in loads:
+        load.start()
     me = lax.axis_index("mem")
     col = lax.axis_index("lon")
     right, left = lax.rem(col + 1, PEERS), lax.rem(col + PEERS - 1, PEERS)
@@ -83,12 +111,12 @@
         pl.semaphore_signal(barrier, inc=1, device_id={"lon": side}, device_id_type=MESH)
     lax.fori_loop(1, PEERS, greet, 0)
 
-    for m in range(2):
-        z_ref[m] = x_ref[m].astype(F32).reshape(1024, 128)
     for buf in (xa_ref, xb_ref, xc_ref):
         buf[0:64, :] = jnp.zeros((64, 384), BF)
         buf[1088:1152, :] = jnp.zeros((64, 384), BF)
+    loads[0].wait()
     for m in range(2):
+        z_ref[m] = x_ref[m].astype(F32).reshape(1024, 128)
         for lat in range(32):
             rows = z_ref[m, pl.ds(lat, 32, stride=32), :]
             xa_ref[64 + 32 * lat : 96 + 32 * lat, 128 * m : 128 * m + 128] = rows.astype(BF)
@@ -115,6 +143,9 @@
     to_left, to_right = halo(0, left), halo(1, right)
     to_left.start()
     to_right.start()
+
+    for load in loads[1:]:
+        load.wait()
 
     for layer, w_ref in enumerate((w1_ref, w2_ref, w3_ref)):
         for dx in range(5):
@@ -180,7 +211,7 @@
                 target[at, 128 * t : 128 * t + 128] = value.astype(BF)
             return carry
 
-        lax.fori_loop(0, 8, body, 0)
+        lax.fori_loop(0, 8, body, 0, unroll=8)
 
     silu_layer(xa_ref, xb_ref, 0)
     silu_layer(xb_ref, xc_ref, 1)
@@ -195,38 +226,31 @@
             device_id_type=MESH,
         )
 
-    def last_layer(step, carry):
-        slot = step // 4
-        quarter = lax.rem(step + me // 4, 4)
-        block = slot * 4 + quarter
-        total = convolve(xc_ref, 2, block)
-        at = pl.ds(pl.multiple_of(64 + block * 128, 64), 128)
-        state = []
-        for t in range(3):
-            value = total[t] + xa_ref[at, 128 * t : 128 * t + 128].astype(F32)
-            state.append(value.astype(BF).astype(F32))
-        lane = iota((128, 128), 1)
-        for m in range(2):
-            low = pltpu.roll(state[2], 112 - 64 * m, 1)
-            high = pltpu.roll(state[2], (80 - 64 * m) % 128, 1)
-            whole = jnp.where(lane < 8, low, jnp.where(lane >= 120, high, state[m]))
-            whole = whole.astype(BF)
-            for row in range(4):
-                send_ref[4 * block + row, m] = whole[32 * row : 32 * row + 32]
-        for row in range(4):
-            peer = quarter * 4 + row
-
-            @pl.when(peer != me)
-            def _():
-                go(slot, peer).start()
-
-            @pl.when(peer == me)
-            def _():
+    def last_layer(slot, carry):
+        for step in range(4):
+            quarter = lax.rem(step + me // 4, 4)
+            block = slot * 4 + quarter
+            total = convolve(xc_ref, 2, block)
+            at = pl.ds(pl.multiple_of(64 + block * 128, 64), 128)
+            state = []
+            for t in range(3):
+                value = total[t] + xa_ref[at, 128 * t : 128 * t + 128].astype(F32)
+                state.append(value.astype(BF).astype(F32))
+            lane = iota((128, 128), 1)
+            for m in range(2):
+                low = pltpu.roll(state[2], 112 - 64 * m, 1)
+                high = pltpu.roll(state[2], (80 - 64 * m) % 128, 1)
+                whole = jnp.where(lane < 8, low, jnp.where(lane >= 120, high, state[m]))
+                whole = whole.astype(BF)
+                for row in range(4):
+                    send_ref[4 * block + row, m] = whole[32 * row : 32 * row + 32]
+            if step == 0:
                 recv_ref[slot, me] = send_ref[16 * slot + me]
-
+            for row in range(1 if step == 0 else 0, 4):
+                go(slot, quarter * 4 + lax.rem(me + row, 4)).start()
         return carry
 
-    lax.fori_loop(0, 8, last_layer, 0)
+    lax.fori_loop(0, 2, last_layer, 0)
 
     scale = math.log2(math.e) / math.sqrt(32 // HEADS)
 
@@ -267,7 +291,7 @@
             v_ref[group] = out[512:768].reshape(32, 8, 128)
             return carry
 
-        lax.fori_loop(0, 4, prepare, 0)
+        lax.fori_loop(0, 4, prepare, 0, unroll=4)
 
         def head(h, carry):
             queries = [[q_ref[mb, 8 * h + d] for mb in range(4)] for d in range(8)]
@@ -311,25 +335,16 @@
 
         lax.fori_loop(0, HEADS, head, 0)
 
-        def finish(group, carry):
+        for step in range(4):
+            group = lax.rem(step + me // 4, 4)
             mixed = mix_ref[group].reshape(256, 128).astype(BF)
             state = recv_ref[slot, pl.ds(4 * group, 4)].astype(F32).reshape(256, 128)
             final = dot(back_ref[...], mixed) + state
             ret_ref[slot, pl.ds(4 * group, 4)] = final.astype(BF).reshape(4, 2, 32, 128)
-            for row in range(4):
-                peer = 4 * group + row
-
-                @pl.when(peer != me)
-                def _():
-                    back(slot, peer).start()
-
-                @pl.when(peer == me)
-                def _():
-                    got_ref[16 * slot + me] = ret_ref[slot, me]
-
-            return carry
-
-        lax.fori_loop(0, 4, finish, 0)
+            if step == 0:
+                got_ref[16 * slot + me] = ret_ref[slot, me]
+            for row in range(1 if step == 0 else 0, 4):
+                back(slot, 4 * group + lax.rem(me + row, 4)).start()
         return carry
 
     lax.fori_loop(0, 2, attend, 0)
@@ -356,7 +371,7 @@
                 ].astype(F32)
             return carry
 
-        lax.fori_loop(0, 16, place, 0)
+        lax.fori_loop(0, 16, place, 0, unroll=16)
         return carry
 
     lax.fori_loop(0, 2, returned, 0)
@@ -379,9 +394,18 @@
     return pl.pallas_call(
         kernel,
         out_shape=jax.ShapeDtypeStruct(members.shape, BF),
-        in_specs=[vmem] * 9,
+        in_specs=[pl.BlockSpec(memory_space=pltpu.HBM)] * 9,
         out_specs=vmem,
         scratch_shapes=[
+            pltpu.VMEM((2, 32, 32, 128), BF),
+            pltpu.VMEM((5, 5, 32, 32), BF),
+            pltpu.VMEM((5, 5, 32, 32), BF),
+            pltpu.VMEM((5, 5, 32, 32), BF),
+            pltpu.VMEM((1, 32), F32),
+            pltpu.VMEM((32, 32), BF),
+            pltpu.VMEM((32, 32), BF),
+            pltpu.VMEM((32, 32), BF),
+            pltpu.VMEM((32, 32), BF),
             pltpu.VMEM((2, 1024, 128), F32),
             pltpu.VMEM((1152, 384), BF),
             pltpu.VMEM((1152, 384), BF),
@@ -407,9 +431,10 @@
             pltpu.SemaphoreType.DMA((2, 16)),
             pltpu.SemaphoreType.DMA((2, 16)),
             pltpu.SemaphoreType.DMA((2, 16)),
+            pltpu.SemaphoreType.DMA((9,)),
         ],
         compiler_params=pltpu.CompilerParams(
-            collective_id=0, has_side_effects=True, vmem_limit_bytes=40 * 1024 * 1024
+            collective_id=0, has_side_effects=True, vmem_limit_bytes=56 * 1024 * 1024
         ),
     )(members, *taps, norm_gain.reshape(1, 32), w_query, w_key, w_value, w_out)
 

time: 53.7 us -> 45 us (0.84)
  local copies, waits for them, and re-layouts: 8.07 us -> 1.87 us
  Pallas kernels: 45.3 us -> 43 us
    unnamed x19 -> x1, local copies, waits for them, and re-layouts: 8.07 us -> 1.87 us
    pallas_call x1, Pallas kernels: 45.3 us -> 43 us  [on_device(): pl.pallas_call(kernel, out_shape=jax.ShapeDtypeStruct(members.shape, BF),...]
where the time goes in v1:
time: 45 us; the launch traced here: 44.9 us
  Pallas kernels  43 us (96%)
  local copies, waits for them, and re-layouts  1.87 us (4%)
    pallas_call x1, Pallas kernels, on_device(): pl.pallas_call(kernel, out_shape=jax.ShapeDtypeStruct(members.shape, BF),...  43 us
    unnamed x1, local copies, waits for them, and re-layouts  1.87 us

profile of v1, /device:TPU:1, one launch (start us, length us, event | category | flops | bytes accessed | tf_op | source)
XLA Modules:
  0.0 44.9 jit_solution(12343086858334587448)
XLA Ops:
  0.0 43.0 %shard_map.91 = bf16[2,32,32,128]{3,2,1,0:T(8,128)(2,1)} custom-call(bf16[2,32,32,128]{3,2,1,0:T(8,128)(2,1)} %x_hbm.1, bf16[5,5,32,32]{3,2,1,0:T(8,128)(2,1)} %bitcast.4, bf16[5,5,32,32]{3,2,1,0:T(8,128)(2,1)} %bitcast.5, bf16[5,5,32,32]{3,2,1,0:T(8,128)(2,1)} %bitcast.6, f32[1,32]{1,0:T(1,128)} %bitcast.7, bf16[32,32]{1,0:T(8,128)(2,1)} %wq_hbm.1, ...), custom_call_target="tpu_custom_call" | custom-call | tf_op jit(solution)/shard_map/pallas_call | solution.py:394
  43.0 1.9 %copy.11 = bf16[2,32,32,128]{3,2,1,0:T(8,128)(2,1)} copy(bf16[2,32,32,128]{3,2,1,0:T(8,128)(2,1)} %shard_map.91) | data formatting | bytes 1048576

commit v2 on v1

v2 whole, which is shorter than its diff:
```python
import math

import jax
import jax.numpy as jnp
from jax import lax
from jax.experimental import pallas as pl
from jax.experimental.pallas import tpu as pltpu
from jax.sharding import PartitionSpec as P

MESH = pl.DeviceIdType.MESH
HEADS = 4
BF = jnp.bfloat16
F32 = jnp.float32
PEERS = 16


def iota(shape, dim):
    return lax.broadcasted_iota(jnp.int32, shape, dim)


def ones_where(mask):
    return jnp.where(mask, 1.0, 0.0).astype(BF)


def dot(a, b, contract=((1,), (0,))):
    return lax.dot_general(a, b, (contract, ((), ())), preferred_element_type=F32)


def device(**where):
    return {name: index for name, index in where.items()}


def kernel(
    x_hbm,
    w1_hbm,
    w2_hbm,
    w3_hbm,
    gain_hbm,
    wq_hbm,
    wk_hbm,
    wv_hbm,
    wo_hbm,
    out_ref,
    x_ref,
    w1_ref,
    w2_ref,
    w3_ref,
    gain_ref,
    wq_ref,
    wk_ref,
    wv_ref,
    wo_ref,
    z_ref,
    xa_ref,
    xb_ref,
    xc_ref,
    band_ref,
    proj_ref,
    back_ref,
    gcol_ref,
    hs_ref,
    hr_ref,
    send_ref,
    recv_ref,
    q_ref,
    k_ref,
    v_ref,
    s_ref,
    mix_ref,
    ret_ref,
    got_ref,
    halo_send,
    halo_recv,
    go_send,
    go_recv,
    back_send,
    back_recv,
    load_sem,
):
    loads = [
        pltpu.make_async_copy(source, target, load_sem.at[index])
        for index, (source, target) in enumerate(
            (
                (x_hbm, x_ref),
                (w1_hbm, w1_ref),
                (w2_hbm, w2_ref),
                (w3_hbm, w3_ref),
                (gain_hbm, gain_ref),
                (wq_hbm, wq_ref),
                (wk_hbm, wk_ref),
                (wv_hbm, wv_ref),
                (wo_hbm, wo_ref),
            )
        )
    ]
    for load in loads:
        load.start()
    me = lax.axis_index("mem")
    col = lax.axis_index("lon")
    right, left = lax.rem(col + 1, PEERS), lax.rem(col + PEERS - 1, PEERS)

    barrier = pltpu.get_barrier_semaphore()

    def greet(step, carry):
        pl.semaphore_signal(
            barrier, inc=1, device_id={"mem": lax.rem(me + step, PEERS)}, device_id_type=MESH
        )
        return carry

    for side in (left, right):
        pl.semaphore_signal(barrier, inc=1, device_id={"lon": side}, device_id_type=MESH)
    lax.fori_loop(1, PEERS, greet, 0)

    for buf in (xa_ref, xb_ref, xc_ref):
        buf[0:64, :] = jnp.zeros((64, 384), BF)
        buf[1088:1152, :] = jnp.zeros((64, 384), BF)
    loads[0].wait()
    for m in range(2):
        z_ref[m] = x_ref[m].astype(F32).reshape(1024, 128)
        for lat in range(32):
            rows = z_ref[m, pl.ds(lat, 32, stride=32), :]
            xa_ref[64 + 32 * lat : 96 + 32 * lat, 128 * m : 128 * m + 128] = rows.astype(BF)

    r, lane = iota((32, 256), 0), iota((32, 256), 1)
    want = jnp.where(r < 16, 0, 120) + (r & 7) + jnp.where((r & 8) != 0, 128, 0)
    edges = dot(ones_where(lane == want), xa_ref[64:1088, 0:256], ((1,), (1,)))
    edges = edges.astype(BF)
    hs_ref[0] = edges[0:16]
    hs_ref[1] = edges[16:32]

    pl.semaphore_wait(barrier, PEERS + 1)

    def halo(side, target):
        return pltpu.make_async_remote_copy(
            src_ref=hs_ref.at[side],
            dst_ref=hr_ref.at[side],
            send_sem=halo_send.at[side],
            recv_sem=halo_recv.at[side],
            device_id={"lon": target},
            device_id_type=MESH,
        )

    to_left, to_right = halo(0, left), halo(1, right)
    to_left.start()
    to_right.start()

    for load in loads[1:]:
        load.wait()

    for layer, w_ref in enumerate((w1_ref, w2_ref, w3_ref)):
        for dx in range(5):
            pieces = [w_ref[dy, dx].astype(F32) for dy in range(5)]
            base = jnp.concatenate(pieces + [jnp.zeros((32, 96), F32)], axis=1)
            for up in range(4):
                rolled = base if up == 0 else pltpu.roll(base, 32 * up, 1)
                at = dx * 128 + up * 32
                band_ref[layer, at : at + 32, :] = rolled.astype(BF)

    def convolve(source, layer, block, tiles):
        rows = pl.ds(pl.multiple_of(block * 128, 128), 256)
        window = source[rows, 128 * tiles[0] : 128 * tiles[-1] + 128]
        total = [None] * len(tiles)
        for dx in range(5):
            y = dot(band_ref[layer, dx * 128 : dx * 128 + 128, :], window)
            for t in range(len(tiles)):
                part = y[:, 128 * t : 128 * t + 128]
                if dx != 2:
                    part = pltpu.roll(part, (2 - dx) % 128, 1)
                total[t] = part if total[t] is None else total[t] + part
        return total

    def silu_layer(source, target, layer, blocks, tiles):
        for block in blocks:
            total = convolve(source, layer, block, tiles)
            for t, value in zip(tiles, total):
                value = 0.5 * value
                value = value * jnp.tanh(value) + value
                at = 64 + 128 * block
                target[at : at + 128, 128 * t : 128 * t + 128] = value.astype(BF)

    def go(slot, peer):
        return pltpu.make_async_remote_copy(
            src_ref=send_ref.at[16 * slot + peer],
            dst_ref=recv_ref.at[slot, me],
            send_sem=go_send.at[slot, peer],
            recv_sem=go_recv.at[slot, me],
            device_id={"mem": peer},
            device_id_type=MESH,
        )

    quarter = me // 4
    half, odd = quarter // 2, lax.rem(quarter, 2)
    order = (2 * (1 - half) + odd, 3 - 2 * half - odd, 2 * half + 1 - odd, quarter)

    def peers_of(step):
        first = 1 if step == 3 else 0
        return [4 * order[step] + lax.rem(me + row, 4) for row in range(first, 4)]

    def residual(block, t, total):
        at = pl.ds(pl.multiple_of(64 + block * 128, 64), 128)
        value = total + xa_ref[at, 128 * t : 128 * t + 128].astype(F32)
        return value.astype(BF)

    silu_layer(xa_ref, xb_ref, 0, range(8), (0, 1))
    silu_layer(xb_ref, xc_ref, 1, range(8), (0, 1))
    for block in range(8):
        total = convolve(xc_ref, 2, block, (0, 1))
        for m in range(2):
            state = residual(block, m, total[m])
            for row in range(4):
                send_ref[4 * block + row, m] = state[32 * row : 32 * row + 32]

    to_left.wait()
    to_right.wait()

    r, lane = iota((256, 128), 0), iota((256, 128), 1)
    lon, base = r & 127, (r >> 7) * 64
    inner = jnp.where(lon < 16, base + 16 + lon, jnp.where(lon >= 112, base + lon - 80, -1))
    r2, lane2 = iota((32, 128), 0), iota((32, 128), 1)
    outer = jnp.where(r2 < 16, 48, 8) + (r2 & 7) + jnp.where((r2 & 8) != 0, 64, 0)
    strip = dot(xa_ref[64:1088, 0:256], ones_where(lane == inner))
    ring = hr_ref[...].reshape(32, 1024)
    strip = strip + dot(ring, ones_where(lane2 == outer), ((0,), (0,)))
    xa_ref[64:1088, 256:384] = strip.astype(BF)

    def edges_and_go(slot):
        for step in range(4):
            block = 4 * slot + order[step]
            strip = residual(block, 2, convolve(xc_ref, 2, block, (2,))[0]).astype(F32)
            lane = iota((128, 128), 1)
            for m in range(2):
                low = pltpu.roll(strip, 112 - 64 * m, 1)
                high = pltpu.roll(strip, (80 - 64 * m) % 128, 1)
                edge = jnp.where(lane < 8, low, high).reshape(4, 32, 128)
                inside = (iota((4, 32, 128), 2) >= 8) & (iota((4, 32, 128), 2) < 120)
                rows = pl.ds(4 * block, 4)
                whole = jnp.where(inside, send_ref[rows, m].astype(F32), edge)
                send_ref[rows, m] = whole.astype(BF)
            if step == 3:
                recv_ref[slot, me] = send_ref[16 * slot + me]
            for peer in peers_of(step):
                go(slot, peer).start()

    silu_layer(xa_ref, xb_ref, 0, range(0, 6), (2,))
    silu_layer(xb_ref, xc_ref, 1, range(0, 5), (2,))
    edges_and_go(0)
    silu_layer(xa_ref, xb_ref, 0, range(6, 8), (2,))
    silu_layer(xb_ref, xc_ref, 1, range(5, 8), (2,))
    edges_and_go(1)

    r, c = iota((256, 32), 0), iota((256, 32), 1)
    spread = ones_where((r >> 3) == c)
    spread_out = ones_where((r & 31) == c)
    c, lane = iota((32, 256), 0), iota((32, 256), 1)
    tile = ones_where((lane & 31) == c)
    tile_out = ones_where((lane >> 3) == c)
    r, lane = iota((256, 256), 0), iota((256, 256), 1)
    own = (r & 7) == (lane >> 5)
    own_out = (r >> 5) == (lane & 7)
    for index, w_ref in enumerate((wq_ref, wk_ref, wv_ref)):
        tall = dot(spread, w_ref[...], ((1,), (1,))).astype(BF)
        full = jnp.where(own, dot(tall, tile), 0.0)
        proj_ref[256 * index : 256 * index + 256, :] = full.astype(BF)
    tall = dot(spread_out, wo_ref[...], ((1,), (1,))).astype(BF)
    back_ref[...] = jnp.where(own_out, dot(tall, tile_out), 0.0).astype(BF)
    eye = iota((32, 32), 0) == iota((32, 32), 1)
    gains = jnp.broadcast_to(gain_ref[...], (32, 32))
    gcol = jnp.sum(jnp.where(eye, gains, 0.0), axis=1, keepdims=True)
    gcol_ref[...] = jnp.broadcast_to(gcol, (32, 128))

    scale = math.log2(math.e) / math.sqrt(32 // HEADS)

    def back(slot, peer):
        return pltpu.make_async_remote_copy(
            src_ref=ret_ref.at[slot, peer],
            dst_ref=got_ref.at[16 * slot + me],
            send_sem=back_send.at[slot, peer],
            recv_sem=back_recv.at[slot, me],
            device_id={"mem": peer},
            device_id_type=MESH,
        )

    def attend(slot, carry):
        for step in (3, 2, 0, 1):
            group = order[step]
            for peer in peers_of(step):
                pltpu.make_async_remote_copy(
                    src_ref=send_ref.at[16 * slot + peer],
                    dst_ref=recv_ref.at[slot, peer],
                    send_sem=go_send.at[slot, peer],
                    recv_sem=go_recv.at[slot, peer],
                    device_id={"mem": peer},
                    device_id_type=MESH,
                ).wait_recv()
            values = recv_ref[slot, pl.ds(4 * group, 4)].astype(F32).reshape(8, 32, 128)
            centred = values - jnp.mean(values, axis=1, keepdims=True)
            spread = jnp.mean(centred * centred, axis=1, keepdims=True)
            normed = centred * lax.rsqrt(spread + 1e-05) * gcol_ref[...][None]
            out = dot(proj_ref[...], normed.astype(BF).reshape(256, 128))
            out = out.astype(BF).astype(F32)
            q_ref[group] = (out[0:256] * scale).reshape(32, 8, 128)
            k_ref[group] = out[256:512].reshape(32, 8, 128)
            v_ref[group] = out[512:768].reshape(32, 8, 128)

        for pair in range(2):
            groups = (order[2 * pair], order[2 * pair + 1])

            def head(h, carry):
                queries = [[q_ref[group, 8 * h + d] for group in groups] for d in range(8)]

                def score(group, peak):
                    peak = list(peak)
                    for n in range(8):
                        total = [None] * 2
                        for d in range(8):
                            key = jnp.broadcast_to(k_ref[group, 8 * h + d, n : n + 1, :], (8, 128))
                            for i in range(2):
                                term = queries[d][i] * key
                                total[i] = term if d == 0 else total[i] + term
                        for i in range(2):
                            s_ref[8 * group + n, i] = total[i]
                            peak[i] = jnp.maximum(peak[i], total[i])
                    return tuple(peak)

                low = jnp.full((8, 128), -jnp.inf, F32)
                peak = lax.fori_loop(0, 4, score, (low,) * 2)

                def mix(group, state):
                    weight, mixed = list(state[0]), [list(m) for m in state[1]]
                    for n in range(8):
                        probs = [jnp.exp2(s_ref[8 * group + n, i] - peak[i]) for i in range(2)]
                        for i in range(2):
                            weight[i] = weight[i] + probs[i]
                        for d in range(8):
                            value = jnp.broadcast_to(
                                v_ref[group, 8 * h + d, n : n + 1, :], (8, 128)
                            )
                            for i in range(2):
                                mixed[d][i] = mixed[d][i] + probs[i] * value
                    return tuple(weight), tuple(tuple(m) for m in mixed)

                zero = jnp.zeros((8, 128), F32)
                weight, mixed = lax.fori_loop(0, 4, mix, ((zero,) * 2, ((zero,) * 2,) * 8))
                for i in range(2):
                    inverse = 1.0 / weight[i]
                    for d in range(8):
                        mix_ref[i, 8 * h + d] = mixed[d][i] * inverse
                return carry

            lax.fori_loop(0, HEADS, head, 0)

            for i in range(2):
                step = 2 * pair + i
                group = order[step]
                mixed = mix_ref[i].reshape(256, 128).astype(BF)
                state = recv_ref[slot, pl.ds(4 * group, 4)].astype(F32).reshape(256, 128)
                final = dot(back_ref[...], mixed) + state
                ret_ref[slot, pl.ds(4 * group, 4)] = final.astype(BF).reshape(4, 2, 32, 128)
                if step == 3:
                    got_ref[16 * slot + me] = ret_ref[slot, me]
                for peer in peers_of(step):
                    back(slot, peer).start()
        return carry

    lax.fori_loop(0, 2, attend, 0)

    def returned(slot, carry):
        for step in range(4):
            for peer in peers_of(step):
                pltpu.make_async_remote_copy(
                    src_ref=ret_ref.at[slot, peer],
                    dst_ref=got_ref.at[16 * slot + peer],
                    send_sem=back_send.at[slot, peer],
                    recv_sem=back_recv.at[slot, peer],
                    device_id={"mem": peer},
                    device_id_type=MESH,
                ).wait_recv()
            for row in range(4):
                lat = 16 * slot + 4 * order[step] + row
                for m in range(2):
                    z_ref[m, pl.ds(lat, 32, stride=32), :] = got_ref[lat, m].astype(F32)
        return carry

    lax.fori_loop(0, 2, returned, 0)
    for m in range(2):
        out_ref[m] = z_ref[m].astype(BF).reshape(32, 32, 128)

    def sent(step, carry):
        peer = lax.rem(me + step, PEERS)
        for slot in range(2):
            go(slot, peer).wait_send()
            back(slot, peer).wait_send()
        return carry

    lax.fori_loop(1, PEERS, sent, 0)


def on_device(members, conv_one, conv_two, conv_three, norm_gain, w_query, w_key, w_value, w_out):
    taps = [jnp.transpose(w, (2, 3, 0, 1)) for w in (conv_one, conv_two, conv_three)]
    vmem = pl.BlockSpec(memory_space=pltpu.VMEM)
    operands = (members, *taps, norm_gain.reshape(1, 32), w_query, w_key, w_value, w_out)
    return pl.pallas_call(
        kernel,
        out_shape=jax.ShapeDtypeStruct(members.shape, BF),
        in_specs=[pl.BlockSpec(memory_space=pltpu.HBM)] * 9,
        out_specs=vmem,
        scratch_shapes=[
            pltpu.VMEM((2, 32, 32, 128), BF),
            pltpu.VMEM((5, 5, 32, 32), BF),
            pltpu.VMEM((5, 5, 32, 32), BF),
            pltpu.VMEM((5, 5, 32, 32), BF),
            pltpu.VMEM((1, 32), F32),
            pltpu.VMEM((32, 32), BF),
            pltpu.VMEM((32, 32), BF),
            pltpu.VMEM((32, 32), BF),
            pltpu.VMEM((32, 32), BF),
            pltpu.VMEM((2, 1024, 128), F32),
            pltpu.VMEM((1152, 384), BF),
            pltpu.VMEM((1152, 384), BF),
            pltpu.VMEM((1152, 384), BF),
            pltpu.VMEM((3, 640, 256), BF),
            pltpu.VMEM((768, 256), BF),
            pltpu.VMEM((256, 256), BF),
            pltpu.VMEM((32, 128), F32),
            pltpu.VMEM((2, 16, 1024), BF),
            pltpu.VMEM((2, 16, 1024), BF),
            pltpu.VMEM((32, 2, 32, 128), BF),
            pltpu.VMEM((2, 16, 2, 32, 128), BF),
            pltpu.VMEM((4, 32, 8, 128), F32),
            pltpu.VMEM((4, 32, 8, 128), F32),
            pltpu.VMEM((4, 32, 8, 128), F32),
            pltpu.VMEM((32, 2, 8, 128), F32),
            pltpu.VMEM((2, 32, 8, 128), F32),
            pltpu.VMEM((2, 16, 2, 32, 128), BF),
            pltpu.VMEM((32, 2, 32, 128), BF),
            pltpu.SemaphoreType.DMA((2,)),
            pltpu.SemaphoreType.DMA((2,)),
            pltpu.SemaphoreType.DMA((2, 16)),
            pltpu.SemaphoreType.DMA((2, 16)),
            pltpu.SemaphoreType.DMA((2, 16)),
            pltpu.SemaphoreType.DMA((2, 16)),
            pltpu.SemaphoreType.DMA((9,)),
        ],
        compiler_params=pltpu.CompilerParams(
            collective_id=0, has_side_effects=True, vmem_limit_bytes=40 * 1024 * 1024
        ),
    )(*[pltpu.with_memory_space_constraint(value, pltpu.HBM) for value in operands])


def solution(mesh):
    in_specs = (P("mem", None, None, "lon"), P(), P(), P(), P(), P(), P(), P(), P())
    out_specs = P("mem", None, None, "lon")
    return jax.shard_map(
        on_device, mesh=mesh, in_specs=in_specs, out_specs=out_specs, check_vma=False
    )
```

time: 45 us -> 41.4 us (0.920)
  Pallas kernels: 43 us -> 40.5 us
  local copies, waits for them, and re-layouts: 1.87 us -> 0.8 us
    pallas_call x1, Pallas kernels: 43 us -> 40.5 us  [on_device(): pl.pallas_call(kernel, out_shape=jax.ShapeDtypeStruct(members.shape, BF),...]
    unnamed x1, local copies, waits for them, and re-layouts: 1.87 us -> 0.8 us
where the time goes in v2:
time: 41.4 us; the launch traced here: 41.3 us
  Pallas kernels  40.5 us (98%)
  local copies, waits for them, and re-layouts  0.8 us (2%)
    pallas_call x1, Pallas kernels, on_device(): pl.pallas_call(kernel, out_shape=jax.ShapeDtypeStruct(members.shape, BF),...  40.5 us

profile of v2, /device:TPU:1, one launch (start us, length us, event | category | flops | bytes accessed | tf_op | source)
XLA Modules:
  0.0 41.3 jit_solution(11901553993821042671)
XLA Ops:
  0.0 40.5 %shard_map.91 = bf16[2,32,32,128]{3,2,1,0:T(8,128)(2,1)S(1)} custom-call(bf16[2,32,32,128]{3,2,1,0:T(8,128)(2,1)} %x_hbm.1, bf16[5,5,32,32]{3,2,1,0:T(8,128)(2,1)} %bitcast.4, bf16[5,5,32,32]{3,2,1,0:T(8,128)(2,1)} %bitcast.5, bf16[5,5,32,32]{3,2,1,0:T(8,128)(2,1)} %bitcast.6, f32[1,32]{1,0:T(1,128)} %bitcast.7, bf16[32,32]{1,0:T(8,128)(2,1)} %wq_hbm.1, ...), custom_call_target="tpu_custom_call" | custom-call | tf_op jit(solution)/shard_map/pallas_call | solution.py:402
  40.5 0.8 %copy.11 = bf16[2,32,32,128]{3,2,1,0:T(8,128)(2,1)} copy(bf16[2,32,32,128]{3,2,1,0:T(8,128)(2,1)S(1)} %shard_map.91) | data formatting | bytes 1048576

commit v3 on v2

--- a/solution.py
+++ b/solution.py
@@ -66,6 +66,12 @@
     k_ref,
     v_ref,
     s_ref,
+    peak_ref,
+    packed_ref,
+    es_ref,
+    er_ref,
+    edges_ref,
+    state_ref,
     mix_ref,
     ret_ref,
     got_ref,
@@ -75,6 +81,8 @@
     go_recv,
     back_send,
     back_recv,
+    edge_send,
+    edge_recv,
     load_sem,
 ):
     loads = [
@@ -201,14 +209,24 @@
         value = total + xa_ref[at, 128 * t : 128 * t + 128].astype(F32)
         return value.astype(BF)
 
-    silu_layer(xa_ref, xb_ref, 0, range(8), (0, 1))
-    silu_layer(xb_ref, xc_ref, 1, range(8), (0, 1))
-    for block in range(8):
-        total = convolve(xc_ref, 2, block, (0, 1))
-        for m in range(2):
-            state = residual(block, m, total[m])
-            for row in range(4):
-                send_ref[4 * block + row, m] = state[32 * row : 32 * row + 32]
+    def main_and_go(slot):
+        for step in range(4):
+            block = 4 * slot + order[step]
+            total = convolve(xc_ref, 2, block, (0, 1))
+            for m in range(2):
+                state = residual(block, m, total[m])
+                send_ref[pl.ds(4 * block, 4), m] = state.reshape(4, 32, 128)
+            if step == 3:
+                recv_ref[slot, me] = send_ref[16 * slot + me]
+            for peer in peers_of(step):
+                go(slot, peer).start()
+
+    silu_layer(xa_ref, xb_ref, 0, range(0, 6), (0, 1))
+    silu_layer(xb_ref, xc_ref, 1, range(0, 5), (0, 1))
+    main_and_go(0)
+    silu_layer(xa_ref, xb_ref, 0, range(6, 8), (0, 1))
+    silu_layer(xb_ref, xc_ref, 1, range(5, 8), (0, 1))
+    main_and_go(1)
 
     to_left.wait()
     to_right.wait()
@@ -223,30 +241,36 @@
     strip = strip + dot(ring, ones_where(lane2 == outer), ((0,), (0,)))
     xa_ref[64:1088, 256:384] = strip.astype(BF)
 
-    def edges_and_go(slot):
-        for step in range(4):
-            block = 4 * slot + order[step]
-            strip = residual(block, 2, convolve(xc_ref, 2, block, (2,))[0]).astype(F32)
-            lane = iota((128, 128), 1)
-            for m in range(2):
-                low = pltpu.roll(strip, 112 - 64 * m, 1)
-                high = pltpu.roll(strip, (80 - 64 * m) % 128, 1)
-                edge = jnp.where(lane < 8, low, high).reshape(4, 32, 128)
-                inside = (iota((4, 32, 128), 2) >= 8) & (iota((4, 32, 128), 2) < 120)
-                rows = pl.ds(4 * block, 4)
-                whole = jnp.where(inside, send_ref[rows, m].astype(F32), edge)
-                send_ref[rows, m] = whole.astype(BF)
-            if step == 3:
-                recv_ref[slot, me] = send_ref[16 * slot + me]
-            for peer in peers_of(step):
-                go(slot, peer).start()
-
-    silu_layer(xa_ref, xb_ref, 0, range(0, 6), (2,))
-    silu_layer(xb_ref, xc_ref, 1, range(0, 5), (2,))
-    edges_and_go(0)
-    silu_layer(xa_ref, xb_ref, 0, range(6, 8), (2,))
-    silu_layer(xb_ref, xc_ref, 1, range(5, 8), (2,))
-    edges_and_go(1)
+    silu_layer(xa_ref, xb_ref, 0, range(8), (2,))
+    silu_layer(xb_ref, xc_ref, 1, range(8), (2,))
+
+    r, lane = iota((512, 128), 0), iota((512, 128), 1)
+    inner, which = r & 127, lane & 31
+    source = (which >> 4) * 64 + jnp.where((which & 8) != 0, 16, 40) + (which & 7)
+    pack = ones_where(((r >> 7) == (lane >> 5)) & (inner == source))
+    for block in range(8):
+        strip = residual(block, 2, convolve(xc_ref, 2, block, (2,))[0]).astype(F32)
+        strip = strip.reshape(4, 4, 8, 128)
+        wide = jnp.concatenate([strip[:, o].reshape(32, 128) for o in range(4)], axis=1)
+        packed_ref[4 * block : 4 * block + 4] = dot(wide.astype(BF), pack).reshape(4, 8, 128)
+    for peer in range(PEERS):
+        both = jnp.concatenate([packed_ref[peer], packed_ref[16 + peer]], axis=0)
+        es_ref[peer] = both.astype(BF)
+
+    def edge(peer):
+        return pltpu.make_async_remote_copy(
+            src_ref=es_ref.at[peer],
+            dst_ref=er_ref.at[me],
+            send_sem=edge_send.at[peer],
+            recv_sem=edge_recv.at[me],
+            device_id={"mem": peer},
+            device_id_type=MESH,
+        )
+
+    er_ref[me] = es_ref[me]
+    for step in range(4):
+        for peer in peers_of(step):
+            edge(peer).start()
 
     r, c = iota((256, 32), 0), iota((256, 32), 1)
     spread = ones_where((r >> 3) == c)
@@ -292,7 +316,18 @@
                     device_id={"mem": peer},
                     device_id_type=MESH,
                 ).wait_recv()
-            values = recv_ref[slot, pl.ds(4 * group, 4)].astype(F32).reshape(8, 32, 128)
+            lane = iota((8, 128), 1)
+            inside = (lane >= 8) & (lane < 120)
+            rows = []
+            for row in range(4):
+                outer = edges_ref[4 * group + row, slot]
+                for m in range(2):
+                    main = recv_ref[slot, 4 * group + row, m].astype(F32)
+                    for o in range(4):
+                        turned = pltpu.roll(outer, (120 - 32 * o - 16 * m) % 128, 1)
+                        rows.append(jnp.where(inside, main[8 * o : 8 * o + 8], turned))
+            values = jnp.concatenate(rows, axis=0).reshape(8, 32, 128)
+            state_ref[group] = values.reshape(256, 128)
             centred = values - jnp.mean(values, axis=1, keepdims=True)
             spread = jnp.mean(centred * centred, axis=1, keepdims=True)
             normed = centred * lax.rsqrt(spread + 1e-05) * gcol_ref[...][None]
@@ -302,65 +337,85 @@
             k_ref[group] = out[256:512].reshape(32, 8, 128)
             v_ref[group] = out[512:768].reshape(32, 8, 128)
 
+        def head_scores(h, carry):
+            queries = [[q_ref[order[i], 8 * h + d] for i in range(4)] for d in range(8)]
+
+            def score(group, peak):
+                peak = list(peak)
+                for n in range(8):
+                    total = [None] * 4
+                    for d in range(8):
+                        key = k_ref[group, 8 * h + d, pl.ds(n, 8, stride=0), :]
+                        for i in range(4):
+                            term = queries[d][i] * key
+                            total[i] = term if d == 0 else total[i] + term
+                    for i in range(4):
+                        s_ref[h, 8 * group + n, i] = total[i]
+                        peak[i] = jnp.maximum(peak[i], total[i])
+                return tuple(peak)
+
+            low = jnp.full((8, 128), -jnp.inf, F32)
+            peak = lax.fori_loop(0, 4, score, (low,) * 4, unroll=2)
+            for i in range(4):
+                peak_ref[h, i] = peak[i]
+            return carry
+
+        lax.fori_loop(0, HEADS, head_scores, 0)
+
         for pair in range(2):
-            groups = (order[2 * pair], order[2 * pair + 1])
-
-            def head(h, carry):
-                queries = [[q_ref[group, 8 * h + d] for group in groups] for d in range(8)]
-
-                def score(group, peak):
-                    peak = list(peak)
-                    for n in range(8):
-                        total = [None] * 2
-                        for d in range(8):
-                            key = jnp.broadcast_to(k_ref[group, 8 * h + d, n : n + 1, :], (8, 128))
-                            for i in range(2):
-                                term = queries[d][i] * key
-                                total[i] = term if d == 0 else total[i] + term
-                        for i in range(2):
-                            s_ref[8 * group + n, i] = total[i]
-                            peak[i] = jnp.maximum(peak[i], total[i])
-                    return tuple(peak)
-
-                low = jnp.full((8, 128), -jnp.inf, F32)
-                peak = lax.fori_loop(0, 4, score, (low,) * 2)
+
+            def head_mix(h, carry):
+                peak = [peak_ref[h, 2 * pair + i] for i in range(2)]
 
                 def mix(group, state):
                     weight, mixed = list(state[0]), [list(m) for m in state[1]]
                     for n in range(8):
-                        probs = [jnp.exp2(s_ref[8 * group + n, i] - peak[i]) for i in range(2)]
+                        probs = [
+                            jnp.exp2(s_ref[h, 8 * group + n, 2 * pair + i] - peak[i])
+                            for i in range(2)
+                        ]
                         for i in range(2):
                             weight[i] = weight[i] + probs[i]
                         for d in range(8):
-                            value = jnp.broadcast_to(
-                                v_ref[group, 8 * h + d, n : n + 1, :], (8, 128)
-                            )
+                            value = v_ref[group, 8 * h + d, pl.ds(n, 8, stride=0), :]
                             for i in range(2):
                                 mixed[d][i] = mixed[d][i] + probs[i] * value
                     return tuple(weight), tuple(tuple(m) for m in mixed)
 
                 zero = jnp.zeros((8, 128), F32)
-                weight, mixed = lax.fori_loop(0, 4, mix, ((zero,) * 2, ((zero,) * 2,) * 8))
+                start = ((zero,) * 2, ((zero,) * 2,) * 8)
+                weight, mixed = lax.fori_loop(0, 4, mix, start, unroll=2)
                 for i in range(2):
                     inverse = 1.0 / weight[i]
                     for d in range(8):
                         mix_ref[i, 8 * h + d] = mixed[d][i] * inverse
                 return carry
 
-            lax.fori_loop(0, HEADS, head, 0)
+            lax.fori_loop(0, HEADS, head_mix, 0)
 
             for i in range(2):
                 step = 2 * pair + i
                 group = order[step]
                 mixed = mix_ref[i].reshape(256, 128).astype(BF)
-                state = recv_ref[slot, pl.ds(4 * group, 4)].astype(F32).reshape(256, 128)
-                final = dot(back_ref[...], mixed) + state
+                final = dot(back_ref[...], mixed) + state_ref[group]
                 ret_ref[slot, pl.ds(4 * group, 4)] = final.astype(BF).reshape(4, 2, 32, 128)
                 if step == 3:
                     got_ref[16 * slot + me] = ret_ref[slot, me]
                 for peer in peers_of(step):
                     back(slot, peer).start()
         return carry
+
+    for step in (3, 2, 0, 1):
+        for peer in peers_of(step):
+            pltpu.make_async_remote_copy(
+                src_ref=es_ref.at[peer],
+                dst_ref=er_ref.at[peer],
+                send_sem=edge_send.at[peer],
+                recv_sem=edge_recv.at[peer],
+                device_id={"mem": peer},
+                device_id_type=MESH,
+            ).wait_recv()
+    edges_ref[...] = er_ref[...].astype(F32).reshape(16, 2, 8, 128)
 
     lax.fori_loop(0, 2, attend, 0)
 
@@ -387,6 +442,7 @@
 
     def sent(step, carry):
         peer = lax.rem(me + step, PEERS)
+        edge(peer).wait_send()
         for slot in range(2):
             go(slot, peer).wait_send()
             back(slot, peer).wait_send()
@@ -429,7 +485,13 @@
             pltpu.VMEM((4, 32, 8, 128), F32),
             pltpu.VMEM((4, 32, 8, 128), F32),
             pltpu.VMEM((4, 32, 8, 128), F32),
-            pltpu.VMEM((32, 2, 8, 128), F32),
+            pltpu.VMEM((4, 32, 4, 8, 128), F32),
+            pltpu.VMEM((4, 4, 8, 128), F32),
+            pltpu.VMEM((32, 8, 128), F32),
+            pltpu.VMEM((16, 16, 128), BF),
+            pltpu.VMEM((16, 16, 128), BF),
+            pltpu.VMEM((16, 2, 8, 128), F32),
+            pltpu.VMEM((4, 256, 128), F32),
             pltpu.VMEM((2, 32, 8, 128), F32),
             pltpu.VMEM((2, 16, 2, 32, 128), BF),
             pltpu.VMEM((32, 2, 32, 128), BF),
@@ -439,6 +501,8 @@
             pltpu.SemaphoreType.DMA((2, 16)),
             pltpu.SemaphoreType.DMA((2, 16)),
             pltpu.SemaphoreType.DMA((2, 16)),
+            pltpu.SemaphoreType.DMA((16,)),
+            pltpu.SemaphoreType.DMA((16,)),
             pltpu.SemaphoreType.DMA((9,)),
         ],
         compiler_params=pltpu.CompilerParams(

time: 41.4 us -> 43.9 us (1.060)
  Pallas kernels: 40.5 us -> 43 us
    pallas_call x1, Pallas kernels: 40.5 us -> 43 us  [on_device(): pl.pallas_call(kernel, out_shape=jax.ShapeDtypeStruct(members.shape, BF),...]
where the time goes in v3:
time: 43.9 us; the launch traced here: 43.8 us
  Pallas kernels  43 us (98%)
  local copies, waits for them, and re-layouts  0.8 us (2%)
    pallas_call x1, Pallas kernels, on_device(): pl.pallas_call(kernel, out_shape=jax.ShapeDtypeStruct(members.shape, BF),...  43 us

profile of v3, /device:TPU:1, one launch (start us, length us, event | category | flops | bytes accessed | tf_op | source)
XLA Modules:
  0.0 43.8 jit_solution(10342525303152786388)
XLA Ops:
  0.0 43.0 %shard_map.91 = bf16[2,32,32,128]{3,2,1,0:T(8,128)(2,1)S(1)} custom-call(bf16[2,32,32,128]{3,2,1,0:T(8,128)(2,1)} %x_hbm.1, bf16[5,5,32,32]{3,2,1,0:T(8,128)(2,1)} %bitcast.4, bf16[5,5,32,32]{3,2,1,0:T(8,128)(2,1)} %bitcast.5, bf16[5,5,32,32]{3,2,1,0:T(8,128)(2,1)} %bitcast.6, f32[1,32]{1,0:T(1,128)} %bitcast.7, bf16[32,32]{1,0:T(8,128)(2,1)} %wq_hbm.1, ...), custom_call_target="tpu_custom_call" | custom-call | tf_op jit(solution)/shard_map/pallas_call | solution.py:458
  43.0 0.8 %copy.11 = bf16[2,32,32,128]{3,2,1,0:T(8,128)(2,1)} copy(bf16[2,32,32,128]{3,2,1,0:T(8,128)(2,1)S(1)} %shard_map.91) | data formatting | bytes 1048576

commit v4 on v2

--- a/solution.py
+++ b/solution.py
@@ -180,7 +180,7 @@
 
     def go(slot, peer):
         return pltpu.make_async_remote_copy(
-            src_ref=send_ref.at[16 * slot + peer],
+            src_ref=send_ref.at[peer, slot],
             dst_ref=recv_ref.at[slot, me],
             send_sem=go_send.at[slot, peer],
             recv_sem=go_recv.at[slot, me],
@@ -201,14 +201,35 @@
         value = total + xa_ref[at, 128 * t : 128 * t + 128].astype(F32)
         return value.astype(BF)
 
+    x_place, y_place, core = me // 8, lax.rem(me // 2, 4), lax.rem(me, 2)
+    chips = [
+        4 * lax.rem(x_place + across, 2) + lax.rem(y_place + along, 4)
+        for across in (1, 0)
+        for along in (2, 1, 3, 0)
+    ]
+
+    def send_chip(slot, step):
+        if step == 7:
+            recv_ref[slot, me] = send_ref[me, slot]
+        else:
+            go(slot, 2 * chips[step] + core).start()
+        go(slot, 2 * chips[step] + 1 - core).start()
+
     silu_layer(xa_ref, xb_ref, 0, range(8), (0, 1))
     silu_layer(xb_ref, xc_ref, 1, range(8), (0, 1))
-    for block in range(8):
+    lane = iota((32, 128), 1)
+    for step in range(8):
+        block = chips[step]
         total = convolve(xc_ref, 2, block, (0, 1))
         for m in range(2):
-            state = residual(block, m, total[m])
-            for row in range(4):
-                send_ref[4 * block + row, m] = state[32 * row : 32 * row + 32]
+            state = residual(block, m, total[m]).astype(F32)
+            for one in range(2):
+                low, high = state[64 * one : 64 * one + 32], state[64 * one + 32 : 64 * one + 64]
+                middle = jnp.where(lane < 64, pltpu.roll(low, 96, 1), pltpu.roll(high, 32, 1))
+                outer = jnp.where(lane < 64, pltpu.roll(low, 32, 1), pltpu.roll(high, 96, 1))
+                send_ref[2 * block + one, 0, m] = middle.astype(BF)
+                send_ref[2 * block + one, 1, m] = outer.astype(BF)
+        send_chip(0, step)
 
     to_left.wait()
     to_right.wait()
@@ -223,30 +244,27 @@
     strip = strip + dot(ring, ones_where(lane2 == outer), ((0,), (0,)))
     xa_ref[64:1088, 256:384] = strip.astype(BF)
 
-    def edges_and_go(slot):
-        for step in range(4):
-            block = 4 * slot + order[step]
-            strip = residual(block, 2, convolve(xc_ref, 2, block, (2,))[0]).astype(F32)
-            lane = iota((128, 128), 1)
-            for m in range(2):
-                low = pltpu.roll(strip, 112 - 64 * m, 1)
-                high = pltpu.roll(strip, (80 - 64 * m) % 128, 1)
-                edge = jnp.where(lane < 8, low, high).reshape(4, 32, 128)
-                inside = (iota((4, 32, 128), 2) >= 8) & (iota((4, 32, 128), 2) < 120)
-                rows = pl.ds(4 * block, 4)
-                whole = jnp.where(inside, send_ref[rows, m].astype(F32), edge)
-                send_ref[rows, m] = whole.astype(BF)
-            if step == 3:
-                recv_ref[slot, me] = send_ref[16 * slot + me]
-            for peer in peers_of(step):
-                go(slot, peer).start()
-
-    silu_layer(xa_ref, xb_ref, 0, range(0, 6), (2,))
-    silu_layer(xb_ref, xc_ref, 1, range(0, 5), (2,))
-    edges_and_go(0)
-    silu_layer(xa_ref, xb_ref, 0, range(6, 8), (2,))
-    silu_layer(xb_ref, xc_ref, 1, range(5, 8), (2,))
-    edges_and_go(1)
+    silu_layer(xa_ref, xb_ref, 0, range(8), (2,))
+    silu_layer(xb_ref, xc_ref, 1, range(8), (2,))
+    lane = iota((32, 128), 1)
+    near = lane & 63
+    inside = (near < 24) | (near >= 40)
+    for step in range(8):
+        block = chips[step]
+        strip = residual(block, 2, convolve(xc_ref, 2, block, (2,))[0]).astype(F32)
+        for m in range(2):
+            for one in range(2):
+                low, high = strip[64 * one : 64 * one + 32], strip[64 * one + 32 : 64 * one + 64]
+                turns = [
+                    pltpu.roll(part, (turn - 64 * m) % 128, 1)
+                    for part, turn in ((low, -16), (low, 16), (high, 48), (high, 80))
+                ]
+                west = jnp.where(lane < 32, turns[0], turns[1])
+                east = jnp.where(lane < 96, turns[2], turns[3])
+                edge = jnp.where(lane < 64, west, east)
+                main = send_ref[2 * block + one, 1, m].astype(F32)
+                send_ref[2 * block + one, 1, m] = jnp.where(inside, main, edge).astype(BF)
+        send_chip(1, step)
 
     r, c = iota((256, 32), 0), iota((256, 32), 1)
     spread = ones_where((r >> 3) == c)
@@ -273,7 +291,7 @@
     def back(slot, peer):
         return pltpu.make_async_remote_copy(
             src_ref=ret_ref.at[slot, peer],
-            dst_ref=got_ref.at[16 * slot + me],
+            dst_ref=got_ref.at[slot, me],
             send_sem=back_send.at[slot, peer],
             recv_sem=back_recv.at[slot, me],
             device_id={"mem": peer},
@@ -285,7 +303,7 @@
             group = order[step]
             for peer in peers_of(step):
                 pltpu.make_async_remote_copy(
-                    src_ref=send_ref.at[16 * slot + peer],
+                    src_ref=send_ref.at[peer, slot],
                     dst_ref=recv_ref.at[slot, peer],
                     send_sem=go_send.at[slot, peer],
                     recv_sem=go_recv.at[slot, peer],
@@ -302,46 +320,45 @@
             k_ref[group] = out[256:512].reshape(32, 8, 128)
             v_ref[group] = out[512:768].reshape(32, 8, 128)
 
-        for pair in range(2):
-            groups = (order[2 * pair], order[2 * pair + 1])
+        for unit in ((0, 1), (2, 3)):
+            count = len(unit)
 
             def head(h, carry):
-                queries = [[q_ref[group, 8 * h + d] for group in groups] for d in range(8)]
+                queries = [[q_ref[order[i], 8 * h + d] for i in unit] for d in range(8)]
 
                 def score(group, peak):
                     peak = list(peak)
                     for n in range(8):
-                        total = [None] * 2
+                        total = [None] * count
                         for d in range(8):
-                            key = jnp.broadcast_to(k_ref[group, 8 * h + d, n : n + 1, :], (8, 128))
-                            for i in range(2):
+                            key = k_ref[group, 8 * h + d, pl.ds(n, 8, stride=0), :]
+                            for i in range(count):
                                 term = queries[d][i] * key
                                 total[i] = term if d == 0 else total[i] + term
-                        for i in range(2):
+                        for i in range(count):
                             s_ref[8 * group + n, i] = total[i]
                             peak[i] = jnp.maximum(peak[i], total[i])
                     return tuple(peak)
 
                 low = jnp.full((8, 128), -jnp.inf, F32)
-                peak = lax.fori_loop(0, 4, score, (low,) * 2)
+                peak = lax.fori_loop(0, 4, score, (low,) * count, unroll=4)
 
                 def mix(group, state):
                     weight, mixed = list(state[0]), [list(m) for m in state[1]]
                     for n in range(8):
-                        probs = [jnp.exp2(s_ref[8 * group + n, i] - peak[i]) for i in range(2)]
-                        for i in range(2):
+                        probs = [jnp.exp2(s_ref[8 * group + n, i] - peak[i]) for i in range(count)]
+                        for i in range(count):
                             weight[i] = weight[i] + probs[i]
                         for d in range(8):
-                            value = jnp.broadcast_to(
-                                v_ref[group, 8 * h + d, n : n + 1, :], (8, 128)
-                            )
-                            for i in range(2):
+                            value = v_ref[group, 8 * h + d, pl.ds(n, 8, stride=0), :]
+                            for i in range(count):
                                 mixed[d][i] = mixed[d][i] + probs[i] * value
                     return tuple(weight), tuple(tuple(m) for m in mixed)
 
                 zero = jnp.zeros((8, 128), F32)
-                weight, mixed = lax.fori_loop(0, 4, mix, ((zero,) * 2, ((zero,) * 2,) * 8))
-                for i in range(2):
+                start = ((zero,) * count, ((zero,) * count,) * 8)
+                weight, mixed = lax.fori_loop(0, 4, mix, start, unroll=4)
+                for i in range(count):
                     inverse = 1.0 / weight[i]
                     for d in range(8):
                         mix_ref[i, 8 * h + d] = mixed[d][i] * inverse
@@ -349,50 +366,57 @@
 
             lax.fori_loop(0, HEADS, head, 0)
 
-            for i in range(2):
-                step = 2 * pair + i
+            for i, step in enumerate(unit):
                 group = order[step]
                 mixed = mix_ref[i].reshape(256, 128).astype(BF)
                 state = recv_ref[slot, pl.ds(4 * group, 4)].astype(F32).reshape(256, 128)
                 final = dot(back_ref[...], mixed) + state
                 ret_ref[slot, pl.ds(4 * group, 4)] = final.astype(BF).reshape(4, 2, 32, 128)
                 if step == 3:
-                    got_ref[16 * slot + me] = ret_ref[slot, me]
+                    got_ref[slot, me] = ret_ref[slot, me]
                 for peer in peers_of(step):
                     back(slot, peer).start()
         return carry
 
     lax.fori_loop(0, 2, attend, 0)
 
-    def returned(slot, carry):
-        for step in range(4):
+    def sent(step, carry):
+        peer = lax.rem(me + step, PEERS)
+        go(0, peer).wait_send()
+        go(1, peer).wait_send()
+        back(0, peer).wait_send()
+        return carry
+
+    lax.fori_loop(1, PEERS, sent, 0)
+
+    lane = iota((32, 128), 1)
+    middle = (lane >= 32) & (lane < 96)
+    for step in range(4):
+        for slot in range(2):
             for peer in peers_of(step):
                 pltpu.make_async_remote_copy(
                     src_ref=ret_ref.at[slot, peer],
-                    dst_ref=got_ref.at[16 * slot + peer],
+                    dst_ref=got_ref.at[slot, peer],
                     send_sem=back_send.at[slot, peer],
                     recv_sem=back_recv.at[slot, peer],
                     device_id={"mem": peer},
                     device_id_type=MESH,
                 ).wait_recv()
-            for row in range(4):
-                lat = 16 * slot + 4 * order[step] + row
-                for m in range(2):
-                    z_ref[m, pl.ds(lat, 32, stride=32), :] = got_ref[lat, m].astype(F32)
-        return carry
-
-    lax.fori_loop(0, 2, returned, 0)
+        for row in range(4):
+            peer = 4 * order[step] + row
+            for m in range(2):
+                inner, outer = got_ref[0, peer, m].astype(F32), got_ref[1, peer, m].astype(F32)
+                low = jnp.where(middle, pltpu.roll(inner, 32, 1), pltpu.roll(outer, 96, 1))
+                high = jnp.where(middle, pltpu.roll(inner, 96, 1), pltpu.roll(outer, 32, 1))
+                z_ref[m, pl.ds(2 * peer, 32, stride=32), :] = low
+                z_ref[m, pl.ds(2 * peer + 1, 32, stride=32), :] = high
+
     for m in range(2):
         out_ref[m] = z_ref[m].astype(BF).reshape(32, 32, 128)
 
-    def sent(step, carry):
-        peer = lax.rem(me + step, PEERS)
-        for slot in range(2):
-            go(slot, peer).wait_send()
-            back(slot, peer).wait_send()
-        return carry
-
-    lax.fori_loop(1, PEERS, sent, 0)
+    for step in range(4):
+        for peer in peers_of(step):
+            back(1, peer).wait_send()
 
 
 def on_device(members, conv_one, conv_two, conv_three, norm_gain, w_query, w_key, w_value, w_out):
@@ -424,15 +448,15 @@
             pltpu.VMEM((32, 128), F32),
             pltpu.VMEM((2, 16, 1024), BF),
             pltpu.VMEM((2, 16, 1024), BF),
-            pltpu.VMEM((32, 2, 32, 128), BF),
+            pltpu.VMEM((16, 2, 2, 32, 128), BF),
             pltpu.VMEM((2, 16, 2, 32, 128), BF),
             pltpu.VMEM((4, 32, 8, 128), F32),
             pltpu.VMEM((4, 32, 8, 128), F32),
             pltpu.VMEM((4, 32, 8, 128), F32),
-            pltpu.VMEM((32, 2, 8, 128), F32),
-            pltpu.VMEM((2, 32, 8, 128), F32),
+            pltpu.VMEM((32, 4, 8, 128), F32),
+            pltpu.VMEM((4, 32, 8, 128), F32),
             pltpu.VMEM((2, 16, 2, 32, 128), BF),
-            pltpu.VMEM((32, 2, 32, 128), BF),
+            pltpu.VMEM((2, 16, 2, 32, 128), BF),
             pltpu.SemaphoreType.DMA((2,)),
             pltpu.SemaphoreType.DMA((2,)),
             pltpu.SemaphoreType.DMA((2, 16)),

time: 41.4 us -> 40.7 us (0.983)
  Pallas kernels: 40.5 us -> 39.8 us
    pallas_call x1, Pallas kernels: 40.5 us -> 39.8 us  [on_device(): pl.pallas_call(kernel, out_shape=jax.ShapeDtypeStruct(members.shape, BF),...]
where the time goes in v4:
time: 40.7 us; the launch traced here: 40.6 us
  Pallas kernels  39.8 us (98%)
  local copies, waits for them, and re-layouts  0.8 us (2%)
    pallas_call x1, Pallas kernels, on_device(): pl.pallas_call(kernel, out_shape=jax.ShapeDtypeStruct(members.shape, BF),...  39.8 us

profile of v4, /device:TPU:1, one launch (start us, length us, event | category | flops | bytes accessed | tf_op | source)
XLA Modules:
  0.0 40.6 jit_solution(8314041377101119386)
XLA Ops:
  0.0 39.8 %shard_map.91 = bf16[2,32,32,128]{3,2,1,0:T(8,128)(2,1)S(1)} custom-call(bf16[2,32,32,128]{3,2,1,0:T(8,128)(2,1)} %x_hbm.1, bf16[5,5,32,32]{3,2,1,0:T(8,128)(2,1)} %bitcast.4, bf16[5,5,32,32]{3,2,1,0:T(8,128)(2,1)} %bitcast.5, bf16[5,5,32,32]{3,2,1,0:T(8,128)(2,1)} %bitcast.6, f32[1,32]{1,0:T(1,128)} %bitcast.7, bf16[32,32]{1,0:T(8,128)(2,1)} %wq_hbm.1, ...), custom_call_target="tpu_custom_call" | custom-call | tf_op jit(solution)/shard_map/pallas_call | solution.py:426
  39.8 0.8 %copy.11 = bf16[2,32,32,128]{3,2,1,0:T(8,128)(2,1)} copy(bf16[2,32,32,128]{3,2,1,0:T(8,128)(2,1)S(1)} %shard_map.91) | data formatting | bytes 1048576

commit v5 on v4

--- a/solution.py
+++ b/solution.py
@@ -112,21 +112,65 @@
     lax.fori_loop(1, PEERS, greet, 0)
 
     for buf in (xa_ref, xb_ref, xc_ref):
-        buf[0:64, :] = jnp.zeros((64, 384), BF)
-        buf[1088:1152, :] = jnp.zeros((64, 384), BF)
+        buf[:, 0:64, :] = jnp.zeros((5, 64, 384), BF)
+        buf[:, 1088:1152, :] = jnp.zeros((5, 64, 384), BF)
     loads[0].wait()
     for m in range(2):
         z_ref[m] = x_ref[m].astype(F32).reshape(1024, 128)
         for lat in range(32):
             rows = z_ref[m, pl.ds(lat, 32, stride=32), :]
-            xa_ref[64 + 32 * lat : 96 + 32 * lat, 128 * m : 128 * m + 128] = rows.astype(BF)
+            xa_ref[2, 64 + 32 * lat : 96 + 32 * lat, 128 * m : 128 * m + 128] = rows.astype(BF)
 
     r, lane = iota((32, 256), 0), iota((32, 256), 1)
     want = jnp.where(r < 16, 0, 120) + (r & 7) + jnp.where((r & 8) != 0, 128, 0)
-    edges = dot(ones_where(lane == want), xa_ref[64:1088, 0:256], ((1,), (1,)))
+    edges = dot(ones_where(lane == want), xa_ref[2, 64:1088, 0:256], ((1,), (1,)))
     edges = edges.astype(BF)
     hs_ref[0] = edges[0:16]
     hs_ref[1] = edges[16:32]
+
+    for load in loads[1:]:
+        load.wait()
+
+    for layer, w_ref in enumerate((w1_ref, w2_ref, w3_ref)):
+        for dx in range(5):
+            pieces = [w_ref[dy, dx].astype(F32) for dy in range(5)]
+            base = jnp.concatenate(pieces + [jnp.zeros((32, 96), F32)], axis=1)
+            for up in range(4):
+                rolled = base if up == 0 else pltpu.roll(base, 32 * up, 1)
+                columns = slice(256 * dx, 256 * dx + 256)
+                band_ref[layer, 32 * up : 32 * up + 32, columns] = rolled.astype(BF)
+
+    def spread_columns(target, rows, t, value):
+        columns = slice(128 * t, 128 * t + 128)
+        for dx in range(5):
+            turned = value if dx == 2 else pltpu.roll(value, (2 - dx) % 128, 1)
+            target[dx, rows, columns] = turned
+
+    def convolve(source, layer, parts):
+        windows = []
+        for block, t in parts:
+            rows = pl.ds(pl.multiple_of(block * 128, 128), 256)
+            columns = slice(128 * t, 128 * t + 128)
+            windows.append(
+                jnp.concatenate([source[dx, rows, columns] for dx in range(5)], axis=0)
+            )
+        y = dot(band_ref[layer], jnp.concatenate(windows, axis=1))
+        return [y[:, 128 * i : 128 * i + 128] for i in range(len(parts))]
+
+    def silu_layer(source, target, layer, pieces):
+        for parts in pieces:
+            for (block, t), value in zip(parts, convolve(source, layer, parts)):
+                value = 0.5 * value
+                value = value * jnp.tanh(value) + value
+                at = 64 + 128 * block
+                spread_columns(target, slice(at, at + 128), t, value.astype(BF))
+
+    own = [((block, 0), (block, 1)) for block in range(8)]
+    strips = [((block, 2), (block + 1, 2)) for block in range(0, 8, 2)]
+
+    for t in range(2):
+        spread_columns(xa_ref, slice(64, 1088), t, xa_ref[2, 64:1088, 128 * t : 128 * t + 128])
+    silu_layer(xa_ref, xb_ref, 0, own[:4])
 
     pl.semaphore_wait(barrier, PEERS + 1)
 
@@ -144,40 +188,6 @@
     to_left.start()
     to_right.start()
 
-    for load in loads[1:]:
-        load.wait()
-
-    for layer, w_ref in enumerate((w1_ref, w2_ref, w3_ref)):
-        for dx in range(5):
-            pieces = [w_ref[dy, dx].astype(F32) for dy in range(5)]
-            base = jnp.concatenate(pieces + [jnp.zeros((32, 96), F32)], axis=1)
-            for up in range(4):
-                rolled = base if up == 0 else pltpu.roll(base, 32 * up, 1)
-                at = dx * 128 + up * 32
-                band_ref[layer, at : at + 32, :] = rolled.astype(BF)
-
-    def convolve(source, layer, block, tiles):
-        rows = pl.ds(pl.multiple_of(block * 128, 128), 256)
-        window = source[rows, 128 * tiles[0] : 128 * tiles[-1] + 128]
-        total = [None] * len(tiles)
-        for dx in range(5):
-            y = dot(band_ref[layer, dx * 128 : dx * 128 + 128, :], window)
-            for t in range(len(tiles)):
-                part = y[:, 128 * t : 128 * t + 128]
-                if dx != 2:
-                    part = pltpu.roll(part, (2 - dx) % 128, 1)
-                total[t] = part if total[t] is None else total[t] + part
-        return total
-
-    def silu_layer(source, target, layer, blocks, tiles):
-        for block in blocks:
-            total = convolve(source, layer, block, tiles)
-            for t, value in zip(tiles, total):
-                value = 0.5 * value
-                value = value * jnp.tanh(value) + value
-                at = 64 + 128 * block
-                target[at : at + 128, 128 * t : 128 * t + 128] = value.astype(BF)
-
     def go(slot, peer):
         return pltpu.make_async_remote_copy(
             src_ref=send_ref.at[peer, slot],
@@ -198,7 +208,7 @@
 
     def residual(block, t, total):
         at = pl.ds(pl.multiple_of(64 + block * 128, 64), 128)
-        value = total + xa_ref[at, 128 * t : 128 * t + 128].astype(F32)
+        value = total + xa_ref[2, at, 128 * t : 128 * t + 128].astype(F32)
         return value.astype(BF)
 
     x_place, y_place, core = me // 8, lax.rem(me // 2, 4), lax.rem(me, 2)
@@ -215,12 +225,12 @@
             go(slot, 2 * chips[step] + core).start()
         go(slot, 2 * chips[step] + 1 - core).start()
 
-    silu_layer(xa_ref, xb_ref, 0, range(8), (0, 1))
-    silu_layer(xb_ref, xc_ref, 1, range(8), (0, 1))
+    silu_layer(xa_ref, xb_ref, 0, own[4:])
+    silu_layer(xb_ref, xc_ref, 1, own)
     lane = iota((32, 128), 1)
     for step in range(8):
         block = chips[step]
-        total = convolve(xc_ref, 2, block, (0, 1))
+        total = convolve(xc_ref, 2, ((block, 0), (block, 1)))
         for m in range(2):
             state = residual(block, m, total[m]).astype(F32)
             for one in range(2):
@@ -239,19 +249,21 @@
     inner = jnp.where(lon < 16, base + 16 + lon, jnp.where(lon >= 112, base + lon - 80, -1))
     r2, lane2 = iota((32, 128), 0), iota((32, 128), 1)
     outer = jnp.where(r2 < 16, 48, 8) + (r2 & 7) + jnp.where((r2 & 8) != 0, 64, 0)
-    strip = dot(xa_ref[64:1088, 0:256], ones_where(lane == inner))
+    strip = dot(xa_ref[2, 64:1088, 0:256], ones_where(lane == inner))
     ring = hr_ref[...].reshape(32, 1024)
     strip = strip + dot(ring, ones_where(lane2 == outer), ((0,), (0,)))
-    xa_ref[64:1088, 256:384] = strip.astype(BF)
-
-    silu_layer(xa_ref, xb_ref, 0, range(8), (2,))
-    silu_layer(xb_ref, xc_ref, 1, range(8), (2,))
+    spread_columns(xa_ref, slice(64, 1088), 2, strip.astype(BF))
+
+    silu_layer(xa_ref, xb_ref, 0, strips)
+    silu_layer(xb_ref, xc_ref, 1, strips)
     lane = iota((32, 128), 1)
     near = lane & 63
     inside = (near < 24) | (near >= 40)
     for step in range(8):
         block = chips[step]
-        strip = residual(block, 2, convolve(xc_ref, 2, block, (2,))[0]).astype(F32)
+        if step % 2 == 0:
+            both = convolve(xc_ref, 2, ((block, 2), (chips[step + 1], 2)))
+        strip = residual(block, 2, both[step % 2]).astype(F32)
         for m in range(2):
             for one in range(2):
                 low, high = strip[64 * one : 64 * one + 32], strip[64 * one + 32 : 64 * one + 64]
@@ -273,14 +285,14 @@
     tile = ones_where((lane & 31) == c)
     tile_out = ones_where((lane >> 3) == c)
     r, lane = iota((256, 256), 0), iota((256, 256), 1)
-    own = (r & 7) == (lane >> 5)
-    own_out = (r >> 5) == (lane & 7)
+    same = (r & 7) == (lane >> 5)
+    same_out = (r >> 5) == (lane & 7)
     for index, w_ref in enumerate((wq_ref, wk_ref, wv_ref)):
         tall = dot(spread, w_ref[...], ((1,), (1,))).astype(BF)
-        full = jnp.where(own, dot(tall, tile), 0.0)
+        full = jnp.where(same, dot(tall, tile), 0.0)
         proj_ref[256 * index : 256 * index + 256, :] = full.astype(BF)
     tall = dot(spread_out, wo_ref[...], ((1,), (1,))).astype(BF)
-    back_ref[...] = jnp.where(own_out, dot(tall, tile_out), 0.0).astype(BF)
+    back_ref[...] = jnp.where(same_out, dot(tall, tile_out), 0.0).astype(BF)
     eye = iota((32, 32), 0) == iota((32, 32), 1)
     gains = jnp.broadcast_to(gain_ref[...], (32, 32))
     gcol = jnp.sum(jnp.where(eye, gains, 0.0), axis=1, keepdims=True)
@@ -439,10 +451,10 @@
             pltpu.VMEM((32, 32), BF),
             pltpu.VMEM((32, 32), BF),
             pltpu.VMEM((2, 1024, 128), F32),
-            pltpu.VMEM((1152, 384), BF),
-            pltpu.VMEM((1152, 384), BF),
-            pltpu.VMEM((1152, 384), BF),
-            pltpu.VMEM((3, 640, 256), BF),
+            pltpu.VMEM((5, 1152, 384), BF),
+            pltpu.VMEM((5, 1152, 384), BF),
+            pltpu.VMEM((5, 1152, 384), BF),
+            pltpu.VMEM((3, 128, 1280), BF),
             pltpu.VMEM((768, 256), BF),
             pltpu.VMEM((256, 256), BF),
             pltpu.VMEM((32, 128), F32),

time: 40.7 us -> 37.4 us (0.919)
  Pallas kernels: 39.8 us -> 36.5 us
    pallas_call x1, Pallas kernels: 39.8 us -> 36.5 us  [on_device(): pl.pallas_call(kernel, out_shape=jax.ShapeDtypeStruct(members.shape, BF),...]
where the time goes in v5:
time: 37.4 us; the launch traced here: 37.3 us
  Pallas kernels  36.5 us (98%)
  local copies, waits for them, and re-layouts  0.8 us (2%)
    pallas_call x1, Pallas kernels, on_device(): pl.pallas_call(kernel, out_shape=jax.ShapeDtypeStruct(members.shape, BF),...  36.5 us
    unnamed x1, local copies, waits for them, and re-layouts  0.8 us

profile of v5, /device:TPU:1, one launch (start us, length us, event | category | flops | bytes accessed | tf_op | source)
XLA Modules:
  0.0 37.3 jit_solution(11720526391435873622)
XLA Ops:
  0.0 36.5 %shard_map.91 = bf16[2,32,32,128]{3,2,1,0:T(8,128)(2,1)S(1)} custom-call(bf16[2,32,32,128]{3,2,1,0:T(8,128)(2,1)} %x_hbm.1, bf16[5,5,32,32]{3,2,1,0:T(8,128)(2,1)} %bitcast.4, bf16[5,5,32,32]{3,2,1,0:T(8,128)(2,1)} %bitcast.5, bf16[5,5,32,32]{3,2,1,0:T(8,128)(2,1)} %bitcast.6, f32[1,32]{1,0:T(1,128)} %bitcast.7, bf16[32,32]{1,0:T(8,128)(2,1)} %wq_hbm.1, ...), custom_call_target="tpu_custom_call" | custom-call | tf_op jit(solution)/shard_map/pallas_call | solution.py:438
  36.5 0.8 %copy.11 = bf16[2,32,32,128]{3,2,1,0:T(8,128)(2,1)} copy(bf16[2,32,32,128]{3,2,1,0:T(8,128)(2,1)S(1)} %shard_map.91) | data formatting | bytes 1048576

commit v6 on v5

--- a/solution.py
+++ b/solution.py
@@ -69,6 +69,7 @@
     mix_ref,
     ret_ref,
     got_ref,
+    strip_ref,
     halo_send,
     halo_recv,
     go_send,
@@ -81,7 +82,8 @@
         pltpu.make_async_copy(source, target, load_sem.at[index])
         for index, (source, target) in enumerate(
             (
-                (x_hbm, x_ref),
+                (x_hbm.at[0], x_ref.at[0]),
+                (x_hbm.at[1], x_ref.at[1]),
                 (w1_hbm, w1_ref),
                 (w2_hbm, w2_ref),
                 (w3_hbm, w3_ref),
@@ -114,8 +116,8 @@
     for buf in (xa_ref, xb_ref, xc_ref):
         buf[:, 0:64, :] = jnp.zeros((5, 64, 384), BF)
         buf[:, 1088:1152, :] = jnp.zeros((5, 64, 384), BF)
-    loads[0].wait()
     for m in range(2):
+        loads[m].wait()
         z_ref[m] = x_ref[m].astype(F32).reshape(1024, 128)
         for lat in range(32):
             rows = z_ref[m, pl.ds(lat, 32, stride=32), :]
@@ -128,7 +130,7 @@
     hs_ref[0] = edges[0:16]
     hs_ref[1] = edges[16:32]
 
-    for load in loads[1:]:
+    for load in loads[2:]:
         load.wait()
 
     for layer, w_ref in enumerate((w1_ref, w2_ref, w3_ref)):
@@ -241,17 +243,38 @@
                 send_ref[2 * block + one, 1, m] = outer.astype(BF)
         send_chip(0, step)
 
-    to_left.wait()
-    to_right.wait()
+    r, c = iota((256, 32), 0), iota((256, 32), 1)
+    spread = ones_where((r >> 3) == c)
+    spread_out = ones_where((r & 31) == c)
+    c, lane = iota((32, 256), 0), iota((32, 256), 1)
+    tile = ones_where((lane & 31) == c)
+    tile_out = ones_where((lane >> 3) == c)
+    r, lane = iota((256, 256), 0), iota((256, 256), 1)
+    same = (r & 7) == (lane >> 5)
+    same_out = (r >> 5) == (lane & 7)
+    for index, w_ref in enumerate((wq_ref, wk_ref, wv_ref)):
+        tall = dot(spread, w_ref[...], ((1,), (1,))).astype(BF)
+        full = jnp.where(same, dot(tall, tile), 0.0)
+        proj_ref[256 * index : 256 * index + 256, :] = full.astype(BF)
+    tall = dot(spread_out, wo_ref[...], ((1,), (1,))).astype(BF)
+    back_ref[...] = jnp.where(same_out, dot(tall, tile_out), 0.0).astype(BF)
+    eye = iota((32, 32), 0) == iota((32, 32), 1)
+    gains = jnp.broadcast_to(gain_ref[...], (32, 32))
+    gcol = jnp.sum(jnp.where(eye, gains, 0.0), axis=1, keepdims=True)
+    gcol_ref[...] = jnp.broadcast_to(gcol, (32, 128))
 
     r, lane = iota((256, 128), 0), iota((256, 128), 1)
     lon, base = r & 127, (r >> 7) * 64
     inner = jnp.where(lon < 16, base + 16 + lon, jnp.where(lon >= 112, base + lon - 80, -1))
     r2, lane2 = iota((32, 128), 0), iota((32, 128), 1)
     outer = jnp.where(r2 < 16, 48, 8) + (r2 & 7) + jnp.where((r2 & 8) != 0, 64, 0)
-    strip = dot(xa_ref[2, 64:1088, 0:256], ones_where(lane == inner))
+    strip_ref[...] = dot(xa_ref[2, 64:1088, 0:256], ones_where(lane == inner))
+    placed = ones_where(lane2 == outer)
+
+    to_left.wait()
+    to_right.wait()
     ring = hr_ref[...].reshape(32, 1024)
-    strip = strip + dot(ring, ones_where(lane2 == outer), ((0,), (0,)))
+    strip = strip_ref[...] + dot(ring, placed, ((0,), (0,)))
     spread_columns(xa_ref, slice(64, 1088), 2, strip.astype(BF))
 
     silu_layer(xa_ref, xb_ref, 0, strips)
@@ -277,26 +300,6 @@
                 main = send_ref[2 * block + one, 1, m].astype(F32)
                 send_ref[2 * block + one, 1, m] = jnp.where(inside, main, edge).astype(BF)
         send_chip(1, step)
-
-    r, c = iota((256, 32), 0), iota((256, 32), 1)
-    spread = ones_where((r >> 3) == c)
-    spread_out = ones_where((r & 31) == c)
-    c, lane = iota((32, 256), 0), iota((32, 256), 1)
-    tile = ones_where((lane & 31) == c)
-    tile_out = ones_where((lane >> 3) == c)
-    r, lane = iota((256, 256), 0), iota((256, 256), 1)
-    same = (r & 7) == (lane >> 5)
-    same_out = (r >> 5) == (lane & 7)
-    for index, w_ref in enumerate((wq_ref, wk_ref, wv_ref)):
-        tall = dot(spread, w_ref[...], ((1,), (1,))).astype(BF)
-        full = jnp.where(same, dot(tall, tile), 0.0)
-        proj_ref[256 * index : 256 * index + 256, :] = full.astype(BF)
-    tall = dot(spread_out, wo_ref[...], ((1,), (1,))).astype(BF)
-    back_ref[...] = jnp.where(same_out, dot(tall, tile_out), 0.0).astype(BF)
-    eye = iota((32, 32), 0) == iota((32, 32), 1)
-    gains = jnp.broadcast_to(gain_ref[...], (32, 32))
-    gcol = jnp.sum(jnp.where(eye, gains, 0.0), axis=1, keepdims=True)
-    gcol_ref[...] = jnp.broadcast_to(gcol, (32, 128))
 
     scale = math.log2(math.e) / math.sqrt(32 // HEADS)
 
@@ -469,13 +472,14 @@
             pltpu.VMEM((4, 32, 8, 128), F32),
             pltpu.VMEM((2, 16, 2, 32, 128), BF),
             pltpu.VMEM((2, 16, 2, 32, 128), BF),
+            pltpu.VMEM((1024, 128), F32),
             pltpu.SemaphoreType.DMA((2,)),
             pltpu.SemaphoreType.DMA((2,)),
             pltpu.SemaphoreType.DMA((2, 16)),
             pltpu.SemaphoreType.DMA((2, 16)),
             pltpu.SemaphoreType.DMA((2, 16)),
             pltpu.SemaphoreType.DMA((2, 16)),
-            pltpu.SemaphoreType.DMA((9,)),
+            pltpu.SemaphoreType.DMA((10,)),
         ],
         compiler_params=pltpu.CompilerParams(
             collective_id=0, has_side_effects=True, vmem_limit_bytes=40 * 1024 * 1024

time: 37.4 us -> 36.6 us (0.979)
  Pallas kernels: 36.5 us -> 35.8 us
    pallas_call x1, Pallas kernels: 36.5 us -> 35.8 us  [on_device(): pl.pallas_call(kernel, out_shape=jax.ShapeDtypeStruct(members.shape, BF),...]
where the time goes in v6:
time: 36.6 us
  Pallas kernels  35.8 us (98%)
  local copies, waits for them, and re-layouts  0.8 us (2%)
    pallas_call x1, Pallas kernels, on_device(): pl.pallas_call(kernel, out_shape=jax.ShapeDtypeStruct(members.shape, BF),...  35.8 us
    unnamed x1, local copies, waits for them, and re-layouts  0.8 us

profile of v6, /device:TPU:1, one launch (start us, length us, event | category | flops | bytes accessed | tf_op | source)
XLA Modules:
  0.0 36.6 jit_solution(3364145097473712559)
XLA Ops:
  0.0 35.8 %shard_map.91 = bf16[2,32,32,128]{3,2,1,0:T(8,128)(2,1)S(1)} custom-call(bf16[2,32,32,128]{3,2,1,0:T(8,128)(2,1)} %x_hbm.1, bf16[5,5,32,32]{3,2,1,0:T(8,128)(2,1)} %bitcast.4, bf16[5,5,32,32]{3,2,1,0:T(8,128)(2,1)} %bitcast.5, bf16[5,5,32,32]{3,2,1,0:T(8,128)(2,1)} %bitcast.6, f32[1,32]{1,0:T(1,128)} %bitcast.7, bf16[32,32]{1,0:T(8,128)(2,1)} %wq_hbm.1, ...), custom_call_target="tpu_custom_call" | custom-call | tf_op jit(solution)/shard_map/pallas_call | solution.py:441
  35.8 0.8 %copy.11 = bf16[2,32,32,128]{3,2,1,0:T(8,128)(2,1)} copy(bf16[2,32,32,128]{3,2,1,0:T(8,128)(2,1)S(1)} %shard_map.91) | data formatting | bytes 1048576

commit v7 on v6

--- a/solution.py
+++ b/solution.py
@@ -118,7 +118,7 @@
         buf[:, 1088:1152, :] = jnp.zeros((5, 64, 384), BF)
     for m in range(2):
         loads[m].wait()
-        z_ref[m] = x_ref[m].astype(F32).reshape(1024, 128)
+        z_ref[m, 0:1024, :] = x_ref[m].astype(F32).reshape(1024, 128)
         for lat in range(32):
             rows = z_ref[m, pl.ds(lat, 32, stride=32), :]
             xa_ref[2, 64 + 32 * lat : 96 + 32 * lat, 128 * m : 128 * m + 128] = rows.astype(BF)
@@ -346,7 +346,8 @@
                     for n in range(8):
                         total = [None] * count
                         for d in range(8):
-                            key = k_ref[group, 8 * h + d, pl.ds(n, 8, stride=0), :]
+                            key = k_ref[group, 8 * h + d, n : n + 1, :]
+                            key = jnp.broadcast_to(key, (8, 128))
                             for i in range(count):
                                 term = queries[d][i] * key
                                 total[i] = term if d == 0 else total[i] + term
@@ -365,7 +366,8 @@
                         for i in range(count):
                             weight[i] = weight[i] + probs[i]
                         for d in range(8):
-                            value = v_ref[group, 8 * h + d, pl.ds(n, 8, stride=0), :]
+                            value = v_ref[group, 8 * h + d, n : n + 1, :]
+                            value = jnp.broadcast_to(value, (8, 128))
                             for i in range(count):
                                 mixed[d][i] = mixed[d][i] + probs[i] * value
                     return tuple(weight), tuple(tuple(m) for m in mixed)
@@ -427,7 +429,7 @@
                 z_ref[m, pl.ds(2 * peer + 1, 32, stride=32), :] = high
 
     for m in range(2):
-        out_ref[m] = z_ref[m].astype(BF).reshape(32, 32, 128)
+        out_ref[m] = z_ref[m, 0:1024, :].astype(BF).reshape(32, 32, 128)
 
     for step in range(4):
         for peer in peers_of(step):
@@ -453,7 +455,7 @@
             pltpu.VMEM((32, 32), BF),
             pltpu.VMEM((32, 32), BF),
             pltpu.VMEM((32, 32), BF),
-            pltpu.VMEM((2, 1024, 128), F32),
+            pltpu.VMEM((2, 1056, 128), F32),
             pltpu.VMEM((5, 1152, 384), BF),
             pltpu.VMEM((5, 1152, 384), BF),
             pltpu.VMEM((5, 1152, 384), BF),

time: 36.6 us -> 36.6 us (level)
  no operation moved by 1% of the time
where the time goes in v7:
time: 36.6 us
  Pallas kernels  35.8 us (98%)
  local copies, waits for them, and re-layouts  0.8 us (2%)
    pallas_call x1, Pallas kernels, on_device(): pl.pallas_call(kernel, out_shape=jax.ShapeDtypeStruct(members.shape, BF),...  35.8 us
    unnamed x1, local copies, waits for them, and re-layouts  0.8 us

profile of v7, /device:TPU:1, one launch (start us, length us, event | category | flops | bytes accessed | tf_op | source)
XLA Modules:
  0.0 36.6 jit_solution(5028050072055225154)
XLA Ops:
  0.0 35.8 %shard_map.91 = bf16[2,32,32,128]{3,2,1,0:T(8,128)(2,1)S(1)} custom-call(bf16[2,32,32,128]{3,2,1,0:T(8,128)(2,1)} %x_hbm.1, bf16[5,5,32,32]{3,2,1,0:T(8,128)(2,1)} %bitcast.4, bf16[5,5,32,32]{3,2,1,0:T(8,128)(2,1)} %bitcast.5, bf16[5,5,32,32]{3,2,1,0:T(8,128)(2,1)} %bitcast.6, f32[1,32]{1,0:T(1,128)} %bitcast.7, bf16[32,32]{1,0:T(8,128)(2,1)} %wq_hbm.1, ...), custom_call_target="tpu_custom_call" | custom-call | tf_op jit(solution)/shard_map/pallas_call | solution.py:443
  35.8 0.8 %copy.11 = bf16[2,32,32,128]{3,2,1,0:T(8,128)(2,1)} copy(bf16[2,32,32,128]{3,2,1,0:T(8,128)(2,1)S(1)} %shard_map.91) | data formatting | bytes 1048576

commit v8 on v7

--- a/solution.py
+++ b/solution.py
@@ -313,7 +313,7 @@
             device_id_type=MESH,
         )
 
-    def attend(slot, carry):
+    def attend(slot, units):
         for step in (3, 2, 0, 1):
             group = order[step]
             for peer in peers_of(step):
@@ -335,7 +335,7 @@
             k_ref[group] = out[256:512].reshape(32, 8, 128)
             v_ref[group] = out[512:768].reshape(32, 8, 128)
 
-        for unit in ((0, 1), (2, 3)):
+        for unit in units:
             count = len(unit)
 
             def head(h, carry):
@@ -393,9 +393,9 @@
                     got_ref[slot, me] = ret_ref[slot, me]
                 for peer in peers_of(step):
                     back(slot, peer).start()
-        return carry
-
-    lax.fori_loop(0, 2, attend, 0)
+
+    attend(0, ((0, 1), (2, 3)))
+    attend(1, ((0, 1), (2,), (3,)))
 
     def sent(step, carry):
         peer = lax.rem(me + step, PEERS)

time: 36.6 us -> 36.6 us (level)
  no operation moved by 1% of the time
where the time goes in v8:
time: 36.6 us; the launch traced here: 36.5 us
  Pallas kernels  35.7 us (98%)
  local copies, waits for them, and re-layouts  0.8 us (2%)
    pallas_call x1, Pallas kernels, on_device(): pl.pallas_call(kernel, out_shape=jax.ShapeDtypeStruct(members.shape, BF),...  35.7 us
    unnamed x1, local copies, waits for them, and re-layouts  0.8 us

profile of v8, /device:TPU:1, one launch (start us, length us, event | category | flops | bytes accessed | tf_op | source)
XLA Modules:
  0.0 36.5 jit_solution(16078331496410151482)
XLA Ops:
  0.0 35.7 %shard_map.91 = bf16[2,32,32,128]{3,2,1,0:T(8,128)(2,1)S(1)} custom-call(bf16[2,32,32,128]{3,2,1,0:T(8,128)(2,1)} %x_hbm.1, bf16[5,5,32,32]{3,2,1,0:T(8,128)(2,1)} %bitcast.4, bf16[5,5,32,32]{3,2,1,0:T(8,128)(2,1)} %bitcast.5, bf16[5,5,32,32]{3,2,1,0:T(8,128)(2,1)} %bitcast.6, f32[1,32]{1,0:T(1,128)} %bitcast.7, bf16[32,32]{1,0:T(8,128)(2,1)} %wq_hbm.1, ...), custom_call_target="tpu_custom_call" | custom-call | tf_op jit(solution)/shard_map/pallas_call | solution.py:443
  35.7 0.8 %copy.11 = bf16[2,32,32,128]{3,2,1,0:T(8,128)(2,1)} copy(bf16[2,32,32,128]{3,2,1,0:T(8,128)(2,1)S(1)} %shard_map.91) | data formatting | bytes 1048576
